TPU v7x, 32 devices: a whole 2x2x4 slice. The times are simulated.
32 devices in a mesh: seq: 8 (over y, x, core), head: 4 (over z).
Axes of the slice: x: 2, y: 2, z: 4, core: 2. Of those that a mesh axis runs over, the one named last changes fastest.
Arguments:
- hidden: bfloat16 [2, 8192, 768], P(None, ('seq', 'head')), may hold values from -6 to 6
- out_grad: bfloat16 [2, 8192, 768], P(None, ('seq', 'head')), may hold values from -6 to 6
- norm_gain: float32 [768], replicated, may hold values from 0.1 to 1.9
- input_projection_weight: bfloat16 [768, 3352], P(('seq', 'head')), may hold values from -0.21875 to 0.21875
- conv_weight: float32 [4, 1792], replicated, may hold values from -3 to 3
- conv_bias: float32 [1792], replicated, may hold values from -3 to 3
- step_bias: float32 [24], replicated, may hold values from -3 to 0
- decay_log: float32 [24], replicated
- skip_weight: float32 [24], replicated, may hold values from 0.5 to 1.5
- gate_gain: float32 [1536], replicated, may hold values from 0.1 to 1.9
- output_projection_weight: bfloat16 [768, 1536], P(('seq', 'head')), may hold values from -0.15625 to 0.15625
Outputs:
- mixed: bfloat16 [2, 8192, 768], P(None, ('seq', 'head'))
- hidden_grad: float32 [2, 8192, 768], P(None, ('seq', 'head'))
- norm_gain_grad: float32 [768], replicated
- in_weight_grad: float32 [768, 3352], P(('seq', 'head'))
- conv_weight_grad: float32 [4, 1792], replicated
- conv_bias_grad: float32 [1792], replicated
- step_bias_grad: float32 [24], replicated
- decay_log_grad: float32 [24], replicated
- skip_weight_grad: float32 [24], replicated
- gate_gain_grad: float32 [1536], replicated
- out_weight_grad: float32 [768, 1536], P(('seq', 'head'))
All inputs are finite; a program needn't handle non-finite values.
Results may differ from a plain program's by a relative error of at most 0.014.
The roundings to bfloat16 on the way count: a program that leaves them out, or rounds other values in their place, can miss the bound.
Values may be sent and summed in bfloat16 or wider, within the bound.
No kernel may reach another device: no remote copies, remote signals or barrier semaphores. Data moves between devices by JAX's collectives and lax.ppermute only.
A program may use at most 192 MiB of HBM per device.

v0:
```python
import jax
import jax.numpy as jnp
from jax import lax
from jax.sharding import PartitionSpec as P

D = 768
H = 24
P_SIZE = 64
N = 128
KERNEL = 4
CH = 256


FULL_ACCURACY = lax.Precision.HIGHEST
EPSILON = 1e-05


def passed_along(x, axis, by):
    count = lax.axis_size(axis)
    pairs = [(i, i + by) for i in range(count) if 0 <= i + by < count]
    return lax.ppermute(x, axis, pairs)


def prefix(x, axis, combine, identity, reverse):
    count, mine = (lax.axis_size(axis), lax.axis_index(axis))
    everything = jax.tree.map(
        lambda part, kind: lax.all_gather(part.astype(kind), axis), x, (jnp.bfloat16, jnp.bfloat16)
    )
    start = jax.tree.map(
        lambda part, zero: jnp.broadcast_to(jnp.asarray(zero, part.dtype), part.shape), x, identity
    )

    def step(k, before):
        at = count - 1 - k if reverse else k
        reached = at > mine if reverse else at < mine
        new = combine(
            before, jax.tree.map(lambda part, own: part[at].astype(own.dtype), everything, x)
        )
        return jax.tree.map(lambda a, b: jnp.where(reached, a, b), new, before)

    return lax.fori_loop(0, count, step, start)


def combine_states(earlier, later):
    return (earlier[0] * later[0], later[0][..., None, None] * earlier[1] + later[1])


def silu_slope(values):
    sigmoid_value = jax.nn.sigmoid(values)
    return sigmoid_value * (1.0 + values * (1.0 - sigmoid_value))


def on_device(
    hidden,
    out_grad,
    norm_gain,
    input_projection_weight,
    conv_weight,
    conv_bias,
    step_bias,
    decay_log,
    skip_weight,
    gate_gain,
    output_projection_weight,
):
    groups = lax.axis_size("head")
    head_index = lax.axis_index("head")
    local_heads = H // groups
    local_inner = local_heads * P_SIZE
    seq_count = hidden.shape[0]
    row_count = hidden.shape[1]
    span_length = row_count * groups
    block_count = span_length // CH
    token_count = seq_count * row_count
    inner_width = gate_gain.shape[0]
    proj_width = input_projection_weight.shape[1]
    widened = hidden.astype(jnp.float32)
    scale_one = lax.rsqrt(jnp.mean(widened * widened, axis=-1, keepdims=True) + EPSILON)
    unit_one = widened * scale_one
    normalized_rows = (unit_one * norm_gain).astype(jnp.bfloat16).reshape(token_count, D)
    in_full, out_full = (
        lax.all_gather(input_projection_weight, ("seq", "head"), axis=0, tiled=True),
        lax.all_gather(output_projection_weight, ("seq", "head"), axis=0, tiled=True),
    )
    projected_features = jnp.dot(normalized_rows, in_full, preferred_element_type=jnp.float32)
    gate_in = projected_features[:, :inner_width]
    remainder = projected_features[:, inner_width:].astype(jnp.bfloat16)
    x_pre = remainder[:, :inner_width].reshape(seq_count, row_count, inner_width)
    bc_pre = remainder[:, inner_width : inner_width + 2 * N]
    step_raw = remainder[:, inner_width + 2 * N :].reshape(seq_count, row_count, H)
    bc_tiled = jnp.tile(bc_pre, (1, groups)).reshape(seq_count, row_count, groups * 2 * N)
    x_span, step_span, bc_span = (
        lax.all_to_all(x_pre, "head", split_axis=2, concat_axis=1, tiled=True),
        lax.all_to_all(step_raw, "head", split_axis=2, concat_axis=1, tiled=True),
        lax.all_to_all(bc_tiled, "head", split_axis=2, concat_axis=1, tiled=True),
    )
    conv_in = jnp.concatenate([x_span, bc_span], axis=2)
    kernel = jnp.concatenate(
        [
            lax.dynamic_slice_in_dim(conv_weight, head_index * local_inner, local_inner, 1),
            conv_weight[:, inner_width:],
        ],
        axis=1,
    )
    conv_offset = jnp.concatenate(
        [
            lax.dynamic_slice_in_dim(conv_bias, head_index * local_inner, local_inner, 0),
            conv_bias[inner_width:],
        ]
    )
    previous = passed_along(conv_in[:, span_length - (KERNEL - 1) :], "seq", 1)
    extended = jnp.concatenate([previous, conv_in], axis=1).astype(jnp.float32)
    conv_pre = conv_offset + kernel[0] * extended[:, 0:span_length]
    for kernel_tap in range(1, KERNEL):
        conv_pre = (
            conv_pre + kernel[kernel_tap] * extended[:, kernel_tap : kernel_tap + span_length]
        )
    conv_out = jax.nn.silu(conv_pre).astype(jnp.bfloat16)
    inputs = conv_out[..., :local_inner].reshape(seq_count, block_count, CH, local_heads, P_SIZE)
    keys_in = conv_out[..., local_inner : local_inner + N].reshape(seq_count, block_count, CH, N)
    queries_in = conv_out[..., local_inner + N :].reshape(seq_count, block_count, CH, N)
    keys_wide = keys_in.astype(jnp.float32)
    queries_wide = queries_in.astype(jnp.float32)
    bias_here = lax.dynamic_slice_in_dim(step_bias, head_index * local_heads, local_heads, 0)
    decay_rate = -jnp.exp(
        lax.dynamic_slice_in_dim(decay_log, head_index * local_heads, local_heads, 0)
    )
    skip_here = lax.dynamic_slice_in_dim(skip_weight, head_index * local_heads, local_heads, 0)
    step_arg = (
        jnp.transpose(
            step_span.reshape(seq_count, block_count, CH, local_heads), (0, 1, 3, 2)
        ).astype(jnp.float32)
        + bias_here[:, None]
    )
    step_sizes = jax.nn.softplus(step_arg)
    cumulative = jnp.cumsum(step_sizes * decay_rate[:, None], axis=-1)
    final_cum = cumulative[..., -1]
    scores = jnp.einsum("sctn,scun->sctu", queries_in, keys_in, preferred_element_type=jnp.float32)
    lower_mask = lax.broadcasted_iota(jnp.int32, (CH, CH), 0) >= lax.broadcasted_iota(
        jnp.int32, (CH, CH), 1
    )
    spread = cumulative[..., :, None] - cumulative[..., None, :]
    decay_mask = jnp.where(lower_mask, jnp.exp(jnp.minimum(spread, 0.0)), 0.0)
    mixing_wide = scores[:, :, None] * decay_mask * step_sizes[..., None, :]
    mixing = mixing_wide.astype(jnp.bfloat16)
    within = jnp.einsum("schtu,scuhp->scthp", mixing, inputs, preferred_element_type=jnp.float32)
    weights = jnp.exp(final_cum[..., None] - cumulative) * step_sizes
    weights_turned = jnp.transpose(weights, (0, 1, 3, 2))
    weighted = (inputs * weights_turned[..., None]).astype(jnp.bfloat16)
    local_state = jnp.einsum(
        "scqhp,scqn->schpn", weighted, keys_in, preferred_element_type=jnp.float32
    )
    block_decay = jnp.exp(final_cum)
    running = jnp.zeros((seq_count, local_heads, P_SIZE, N), jnp.float32)
    start_list = []
    for block_at in range(block_count):
        start_list.append(running)
        running = block_decay[:, block_at][..., None, None] * running + local_state[:, block_at]
    local_starts = jnp.stack(start_list, axis=1)
    device_decay = jnp.exp(jnp.sum(final_cum, axis=1))
    identity = (jnp.ones_like(device_decay), jnp.zeros_like(running))
    incoming_decay, incoming = prefix(
        (device_decay, running), "seq", combine_states, identity, False
    )
    before_sum = jnp.cumsum(final_cum, axis=1) - final_cum
    starts = local_starts + jnp.exp(before_sum)[..., None, None] * incoming[:, None]
    exp_turned = jnp.transpose(jnp.exp(cumulative), (0, 1, 3, 2))
    carried = (
        jnp.einsum("scqn,schpn->scqhp", queries_wide, starts, precision=FULL_ACCURACY)
        * exp_turned[..., None]
    )
    mixed_heads = within + carried + skip_here[:, None] * inputs
    mixed_low = mixed_heads.reshape(seq_count, span_length, local_inner).astype(jnp.bfloat16)
    mixed_tokens = lax.all_to_all(mixed_low, "head", split_axis=1, concat_axis=2, tiled=True)
    gate_wide = gate_in.reshape(seq_count, row_count, inner_width)
    gate_act = jax.nn.silu(gate_wide)
    mixed_values = mixed_tokens.astype(jnp.float32)
    gated_values = mixed_values * gate_act
    scale_two = lax.rsqrt(jnp.mean(gated_values * gated_values, axis=-1, keepdims=True) + EPSILON)
    unit_two = gated_values * scale_two
    mixer_input_rows = (unit_two * gate_gain).astype(jnp.bfloat16).reshape(token_count, inner_width)
    branch_output = lax.dot_general(
        mixer_input_rows, out_full, (((1,), (1,)), ((), ())), preferred_element_type=jnp.float32
    )
    mixed = (widened + branch_output.reshape(seq_count, row_count, D)).astype(jnp.bfloat16)
    in_back, out_back = (
        lax.all_gather(input_projection_weight, ("seq", "head"), axis=0, tiled=True),
        lax.all_gather(output_projection_weight, ("seq", "head"), axis=0, tiled=True),
    )
    cotangent = out_grad.reshape(token_count, D)
    d_mixed_in = jnp.dot(cotangent, out_back, preferred_element_type=jnp.float32).reshape(
        seq_count, row_count, inner_width
    )
    gate_gain_part = jnp.sum(d_mixed_in * unit_two, axis=(0, 1))
    d_unit_two = d_mixed_in * gate_gain
    d_gated = scale_two * (
        d_unit_two - unit_two * jnp.mean(d_unit_two * unit_two, axis=-1, keepdims=True)
    )
    d_mixed_low = (d_gated * gate_act).astype(jnp.bfloat16)
    d_gate = d_gated * mixed_values * silu_slope(gate_wide)
    d_heads = lax.all_to_all(d_mixed_low, "head", split_axis=2, concat_axis=1, tiled=True)
    d_output = d_heads.reshape(seq_count, block_count, CH, local_heads, P_SIZE)
    d_wide = d_output.astype(jnp.float32)
    skip_part = jnp.sum(d_wide * inputs, axis=(0, 1, 2, 4))
    d_inputs = skip_here[:, None] * d_wide
    d_mixing = jnp.einsum(
        "scthp,scuhp->schtu", d_output, inputs, preferred_element_type=jnp.float32
    )
    d_inputs = d_inputs + jnp.einsum(
        "schtu,scthp->scuhp", mixing, d_output, preferred_element_type=jnp.float32
    )
    effect = d_mixing * mixing_wide
    d_cum = jnp.sum(effect, axis=-1) - jnp.sum(effect, axis=-2)
    d_steps = jnp.sum(d_mixing * scores[:, :, None] * decay_mask, axis=-2)
    d_scores = jnp.sum(d_mixing * decay_mask * step_sizes[..., None, :], axis=2)
    d_queries = jnp.einsum("sctu,scun->sctn", d_scores, keys_wide, precision=FULL_ACCURACY)
    d_keys = jnp.einsum("sctu,sctn->scun", d_scores, queries_wide, precision=FULL_ACCURACY)
    scaled_grad = d_wide * exp_turned[..., None]
    state_terms = jnp.einsum(
        "scqhp,scqn->schpn", scaled_grad, queries_wide, precision=FULL_ACCURACY
    )
    running_back = jnp.zeros((seq_count, local_heads, P_SIZE, N), jnp.float32)
    after_list = [running_back] * block_count
    for block_at in range(block_count - 1, -1, -1):
        after_list[block_at] = running_back
        running_back = (
            state_terms[:, block_at] + block_decay[:, block_at][..., None, None] * running_back
        )
    local_after = jnp.stack(after_list, axis=1)
    incoming_back_decay, incoming_back = prefix(
        (device_decay, running_back), "seq", combine_states, identity, True
    )
    after_sum = jnp.sum(final_cum, axis=1, keepdims=True) - jnp.cumsum(final_cum, axis=1)
    d_after = local_after + jnp.exp(after_sum)[..., None, None] * incoming_back[:, None]
    d_weighted = jnp.einsum("schpn,scqn->scqhp", d_after, keys_wide, precision=FULL_ACCURACY)
    d_keys = d_keys + jnp.einsum(
        "scqhp,schpn->scqn", weighted.astype(jnp.float32), d_after, precision=FULL_ACCURACY
    )
    d_inputs = d_inputs + d_weighted * weights_turned[..., None]
    d_weights = jnp.transpose(jnp.sum(d_weighted * inputs, axis=-1), (0, 1, 3, 2))
    weight_effect = d_weights * weights
    d_steps = d_steps + d_weights * jnp.exp(final_cum[..., None] - cumulative)
    d_final = jnp.sum(weight_effect, axis=-1) + block_decay * jnp.sum(
        starts * d_after, axis=(-2, -1)
    )
    d_queries = d_queries + jnp.einsum(
        "scqhp,schpn->scqn", scaled_grad, starts, precision=FULL_ACCURACY
    )
    d_cum = d_cum - weight_effect + jnp.transpose(jnp.sum(d_wide * carried, axis=-1), (0, 1, 3, 2))
    d_cum = d_cum.at[..., -1].add(d_final)
    d_decay_step = jnp.flip(jnp.cumsum(jnp.flip(d_cum, -1), axis=-1), -1)
    d_steps = d_steps + d_decay_step * decay_rate[:, None]
    decay_part = jnp.sum(d_decay_step * step_sizes, axis=(0, 1, 3)) * decay_rate
    d_step_arg = d_steps * jax.nn.sigmoid(step_arg)
    bias_part = jnp.sum(d_step_arg, axis=(0, 1, 3))
    d_step_low = (
        jnp.transpose(d_step_arg, (0, 1, 3, 2))
        .reshape(seq_count, span_length, local_heads)
        .astype(jnp.bfloat16)
    )
    d_conv_out = jnp.concatenate(
        [
            d_inputs.reshape(seq_count, span_length, local_inner),
            d_keys.reshape(seq_count, span_length, N),
            d_queries.reshape(seq_count, span_length, N),
        ],
        axis=2,
    )
    d_conv_pre = d_conv_out * silu_slope(conv_pre)
    following = passed_along(d_conv_pre[:, : KERNEL - 1], "seq", -1)
    d_extended = jnp.concatenate([d_conv_pre, following], axis=1)
    d_conv_in = kernel[0] * d_extended[:, KERNEL - 1 : KERNEL - 1 + span_length]
    for kernel_tap in range(1, KERNEL):
        d_conv_in = (
            d_conv_in
            + kernel[kernel_tap]
            * d_extended[:, KERNEL - 1 - kernel_tap : KERNEL - 1 - kernel_tap + span_length]
        )
    kernel_part = jnp.stack(
        [
            jnp.sum(d_conv_pre * extended[:, kernel_tap : kernel_tap + span_length], axis=(0, 1))
            for kernel_tap in range(KERNEL)
        ]
    )
    offset_part = jnp.sum(d_conv_pre, axis=(0, 1))
    d_x_low = d_conv_in[..., :local_inner].astype(jnp.bfloat16)
    d_bc_low = d_conv_in[..., local_inner:].astype(jnp.bfloat16)
    d_x_tok, d_step_tok, d_bc_tok = (
        lax.all_to_all(d_x_low, "head", split_axis=1, concat_axis=2, tiled=True),
        lax.all_to_all(d_step_low, "head", split_axis=1, concat_axis=2, tiled=True),
        lax.all_to_all(d_bc_low, "head", split_axis=1, concat_axis=2, tiled=True),
    )
    d_bc_sum = jnp.sum(
        d_bc_tok.astype(jnp.float32).reshape(seq_count, row_count, groups, 2 * N), axis=2
    )
    d_projected = (
        jnp.concatenate(
            [d_gate, d_x_tok.astype(jnp.float32), d_bc_sum, d_step_tok.astype(jnp.float32)], axis=2
        )
        .astype(jnp.bfloat16)
        .reshape(token_count, proj_width)
    )
    d_normed = lax.dot_general(
        d_projected, in_back, (((1,), (1,)), ((), ())), preferred_element_type=jnp.float32
    ).reshape(seq_count, row_count, D)
    norm_part = jnp.sum(d_normed * unit_one, axis=(0, 1))
    d_unit_one = d_normed * norm_gain
    hidden_grad = out_grad.astype(jnp.float32) + scale_one * (
        d_unit_one - unit_one * jnp.mean(d_unit_one * unit_one, axis=-1, keepdims=True)
    )
    in_term = lax.dot_general(
        normalized_rows, d_projected, (((0,), (0,)), ((), ())), preferred_element_type=jnp.float32
    )
    out_term = lax.dot_general(
        cotangent, mixer_input_rows, (((0,), (0,)), ((), ())), preferred_element_type=jnp.float32
    )
    weight_rows = lax.psum_scatter(
        jnp.concatenate([in_term, out_term], axis=1),
        ("seq", "head"),
        scatter_dimension=0,
        tiled=True,
    )
    kernel_full = lax.dynamic_update_slice_in_dim(
        jnp.zeros(conv_weight.shape, jnp.float32),
        kernel_part[:, :local_inner],
        head_index * local_inner,
        1,
    )
    kernel_full = kernel_full.at[:, inner_width:].set(kernel_part[:, local_inner:])
    offset_full = lax.dynamic_update_slice_in_dim(
        jnp.zeros(conv_bias.shape, jnp.float32),
        offset_part[:local_inner],
        head_index * local_inner,
        0,
    )
    offset_full = offset_full.at[inner_width:].set(offset_part[local_inner:])
    bias_full = lax.dynamic_update_slice_in_dim(
        jnp.zeros((H,), jnp.float32), bias_part, head_index * local_heads, 0
    )
    decay_full = lax.dynamic_update_slice_in_dim(
        jnp.zeros((H,), jnp.float32), decay_part, head_index * local_heads, 0
    )
    skip_full = lax.dynamic_update_slice_in_dim(
        jnp.zeros((H,), jnp.float32), skip_part, head_index * local_heads, 0
    )
    summed_grads = lax.psum(
        (norm_part, kernel_full, offset_full, bias_full, decay_full, skip_full, gate_gain_part),
        ("seq", "head"),
    )
    return (
        mixed,
        hidden_grad,
        summed_grads[0],
        weight_rows[:, :proj_width],
        summed_grads[1],
        summed_grads[2],
        summed_grads[3],
        summed_grads[4],
        summed_grads[5],
        summed_grads[6],
        weight_rows[:, proj_width:],
    )


def solution(mesh):
    placed = (
        P(None, ("seq", "head"), None),
        P(None, ("seq", "head"), None),
        P(),
        P(("seq", "head"), None),
        P(),
        P(),
        P(),
        P(),
        P(),
        P(),
        P(("seq", "head"), None),
    )
    return jax.shard_map(
        on_device,
        mesh=mesh,
        in_specs=placed,
        out_specs=(
            P(None, ("seq", "head"), None),
            P(None, ("seq", "head"), None),
            P(),
            P(("seq", "head"), None),
            P(),
            P(),
            P(),
            P(),
            P(),
            P(),
            P(("seq", "head"), None),
        ),
        check_vma=False,
    )
```

profile of v0, /device:TPU:0, one launch (start us, length us, event | category | flops | bytes accessed | tf_op | source)
XLA Modules:
  0.0 896.7 jit_solution(14452288180772130444)
XLA Ops:
  12.1 67.1 %all-gather.7.cloned.1.call-done = bf16[768,3352]{1,0:T(8,128)(2,1)} async-done(((bf16[24,3352]{1,0:T(8,128)(2,1)}), bf16[768,3352]{1,0:T(8,128)(2,1)}) %all-gather.7.cloned.1.call-update) | async-done | bytes 5148688 | tf_op jit(solution)/shard_map/all_gather | solution.py:82
  79.2 8.5 fusion.121
  88.4 3.5 all-to-all-start.2
  99.1 3.6 copy.530
  102.8 5.1 all-to-all-start.1
  109.1 3.6 reshape.451
  112.7 20.9 %all-to-all-done.1 = bf16[2,256,1024]{1,0,2:T(2,128)(2,1)} async-done(((bf16[2,256,1024]{1,0,2:T(2,128)(2,1)}), bf16[2,256,1024]{1,0,2:T(2,128)(2,1)}, u32[]{:S(2)}, u32[]{:S(2)}) %all-to-all-start.1) | async-done | bytes 1048608 | tf_op jit(solution)/shard_map/all_to_all | solution.py:95
  133.6 4.3 all-to-all-start
  142.9 14.4 %reduce-window.14 = f32[2,4,6,2,128]{4,3,2,1,0:T(2,128)S(1)} reduce-window(f32[2,4,6,2,128]{4,3,2,1,0:T(2,128)S(1)} %copy.538, f32[]{:T(128)} %constant.187.clone.1), window={size=1x1x1x1x128 pad=0_0x0_0x0_0x0_0x127_0}, to_apply=%region_1.2 | reduce-window | flops 1560576 | bytes 98308 | tf_op jit(solution)/shard_map/reduce-window
  165.6 8.9 all-to-all-done
  174.5 3.8 copy.711
  178.2 2.8 all_to_all.35
  185.2 2.6 maximum_convert_fusion
  187.8 6.2 multiply_convert_fusion
  195.0 2.7 slice_convert_fusion
  198.0 3.1 reshape.452
  211.8 15.5 %all-gather.1 = bf16[8,2,6]{2,1,0:T(2,128)(2,1)} all-gather(bf16[1,2,6]{2,1,0:T(2,128)(2,1)S(1)} %bitcast.335), channel_id=2, replica_groups=mesh['seq'=8,'head'=4] {'seq'}, dimensions={0}, use_global_device_ids=true | all-gather | bytes 216 | tf_op jit(solution)/shard_map/all_gather | solution.py:27
  234.8 13.7 %while.33 = (s32[]{:T(128)}, f32[2,6,64,128]{3,2,1,0:T(8,128)S(1)}, s32[]{:T(128)}, bf16[8,2,6]{2,1,0:T(2,128)(2,1)}, bf16[8,2,6,64,128]{4,3,2,1,0:T(8,128)(2,1)}, /*index=5*/s32[]{:T(128)}, s32[]{:T(128)}) while((s32[]{:T(128)}, f32[2,6,64,128]{3,2,1,0:T(8,128)S(1)}, s32[]{:T(128)}, bf16[8,2,6]{2,1,0:T(2,128)(2,1)}, ...), condition=%wide.region_6.7_spmd.clone, body=%wide.region_5.6_spmd.clone.sunk | while | flops 491536 | bytes 983273 | solution.py:41
  251.9 4.9 fusion.23
  259.2 2.9 copy.559
  262.1 4.6 all-to-all-start.3
  268.8 3.4 reshape.458
  274.6 4.0 copy.563
  278.6 33.1 %all-to-all-done.3 = bf16[2,1024,384]{2,0,1:T(2,128)(2,1)} async-done(((bf16[2,1024,384]{2,0,1:T(2,128)(2,1)}), bf16[2,1024,384]{2,0,1:T(2,128)(2,1)}, u32[]{:S(2)}, u32[]{:S(2)}) %all-to-all-start.3) | async-done | bytes 1572896 | tf_op jit(solution)/shard_map/all_to_all | solution.py:174
  311.8 3.6 convert_bitcast_fusion
  319.4 8.2 multiply_reduce_fusion.6
  327.6 3.1 multiply_convert_fusion.3
  330.7 2.9 copy.569
  333.6 3.7 all-to-all-start.4
  337.4 37.1 %all-to-all-done.4 = bf16[2,256,1536]{1,0,2:T(2,128)(2,1)S(1)} async-done(((bf16[2,256,1536]{1,0,2:T(2,128)(2,1)}), bf16[2,256,1536]{1,0,2:T(2,128)(2,1)S(1)}, u32[]{:S(2)}, u32[]{:S(2)}) %all-to-all-start.4) | async-done | bytes 1572896 | tf_op jit(solution)/shard_map/all_to_all | solution.py:201
  385.9 12.8 %fusion.4 = (f32[2,4,6,256]{3,2,1,0:T(8,128)S(1)}, f32[2,4,6,256]{3,2,1,0:T(8,128)S(1)}, f32[2,4,6,256]{3,2,1,0:T(8,128)}, f32[2,4,256,256]{3,2,1,0:T(8,128)}) fusion(f32[2,4,6,256]{3,2,1,0:T(8,128)S(1)} %copy-done.40, f32[2,4,6,256]{3,2,1,0:T(8,128)S(1)} %copy-done.43, f32[2,4,256,256]{3,2,1,0:T(8,128)} %fusion.122, pred[256,256]{1,0:T(8,128)(4,1)S(1)} %copy-done.46, ...), kind=kOutput, calls=%fused_computation.16 | convolution fusion | flops 446132224 | bytes 7651328 | tf_op jit(solution)/shard_map/scthp,scuhp->schtu/dot_general | solution.py:206
  401.4 7.4 fusion.63
  416.0 13.9 %while.34 = (s32[]{:T(128)}, f32[2,6,64,128]{3,2,1,0:T(8,128)S(1)}, s32[]{:T(128)}, bf16[8,2,6]{2,1,0:T(2,128)(2,1)}, bf16[8,2,6,64,128]{4,3,2,1,0:T(8,128)(2,1)...) while((s32[]{:T(128)}, f32[2,6,64,128]{3,2,1,0:T(8,128)S(1)}, s32[]{:T(128)}, ...), condition=%wide.region_10.11_spmd.clone, body=%wide.region_9.10_spmd.clone.sunk | while | flops 491540 | bytes 983335 | solution.py:41
  429.9 3.1 multiply_reduce_fusion.9
  433.0 3.2 fusion.24
  436.2 2.7 fusion.66
  440.3 4.8 fusion.86
  450.7 14.4 %reduce-window.16 = f32[2,4,6,2,128]{4,3,2,1,0:T(2,128)S(1)} reduce-window(f32[2,4,6,2,128]{4,3,2,1,0:T(2,128)S(1)} %copy.602, f32[]{:T(128)} %constant.187.clone.1), window={size=1x1x1x1x128 pad=0_0x0_0x0_0x0_0x127_0}, to_apply=%region_20.21 | reduce-window | flops 1560576 | bytes 98308 | tf_op jit(solution)/shard_map/reduce-window.2
  467.1 3.2 multiply_reduce_fusion.10
  473.4 3.7 convolution_add_fusion.1
  478.5 7.4 fusion.26
  485.9 3.7 copy.578
  489.6 5.2 reshape.461
  494.8 15.0 %multiply_reduce_fusion.5 = (f32[640]{0:T(1024)}, f32[640]{0:T(1024)}, f32[640]{0:T(1024)}, f32[640]{0:T(1024)}, f32[640]{0:T(1024)}, /*index=5*/f32[2,1024,640]{1,2,0:T(8,128)S(1)}) fusion(f32[2,1027,640]{1,2,0:T(8,128)} %copy-done, f32[2,1024,640]{1,2,0:T(8,128)} %get-tuple-element.457, f32[2,1024,128]{1,2,0:T(8,128)} %copy.584, ...), kind=kLoop, calls=%fused_computation.36 | loop fusion | flops 24900480 | bytes 36712960 | tf_op jit(solution)/shard_map/reduce_sum | solution.py:281
  516.3 3.3 all-to-all-start.7
  519.8 11.2 %fusion.13 = bf16[2,1024,640]{1,2,0:T(8,128)(2,1)S(1)} fusion(f32[2,1024,640]{1,2,0:T(8,128)} %copy-done.1, f32[2,3,640]{1,2,0:T(8,128)S(1)} %copy.586, f32[640]{0:T(1024)S(1)} %get-tuple-element.414, f32[640]{0:T(1024)S(1)} %copy-done.50, f32[640]{0:T(1024)S(1)} %get-tuple-element.413, f32[640]{0:T(1024)S(1)} %get-tuple-element.412), kind=kLoop, calls=%fused_computation.27 | loop fusion | flops 14417920 | bytes 7889920 | tf_op jit(solution)/shard_map/convert.26
  534.6 5.1 all-to-all-start.6
  539.7 2.7 slice.301
  542.4 5.1 copy.587
  547.5 19.0 %all-to-all-done.6 = bf16[2,1024,256]{2,0,1:T(2,128)(2,1)S(1)} async-done(((bf16[2,1024,256]{2,0,1:T(2,128)(2,1)}), bf16[2,1024,256]{2,0,1:T(2,128)(2,1)S(1)}, u32[]{:S(2)}, u32[]{:S(2)}) %all-to-all-start.6) | async-done | bytes 1048608 | tf_op jit(solution)/shard_map/all_to_all | solution.py:291
  566.4 4.4 all-to-all-start.5
  571.0 7.1 convolution_bitcast_fusion.1
  581.3 26.7 %all-to-all-done.5 = bf16[2,1024,384]{2,0,1:T(2,128)(2,1)} async-done(((bf16[2,1024,384]{2,0,1:T(2,128)(2,1)}), bf16[2,1024,384]{2,0,1:T(2,128)(2,1)}, u32[]{:S(2)}, u32[]{:S(2)}) %all-to-all-start.5) | async-done | bytes 1572896 | tf_op jit(solution)/shard_map/all_to_all | solution.py:289
  608.1 3.8 copy.710
  611.9 3.9 convert_element_type.252
  615.8 5.1 convolution_bitcast_fusion
  620.9 5.7 pad_maximum_fusion
  626.7 5.9 copy.561
  634.8 3.8 multiply_convert_fusion.4
  638.6 2.7 copy.636
  641.3 4.6 fusion.51
  648.9 7.4 fusion.49
  656.4 40.0 %all-reduce.1 = (f32[768]{0:T(1024)}, f32[4,1792]{1,0:T(4,128)}, f32[1792]{0:T(1024)}, f32[24]{0:T(128)}, f32[24]{0:T(128)}, /*index=5*/f32[24]{0:T(128)}, f32[1536]{0:T(1024)}) all-reduce(f32[768]{0:T(1024)} %get-tuple-element.410, f32[4,1792]{1,0:T(4,128)} %copy-done.36, ...), channel_id=1, replica_groups=mesh['seq'=8,'head'=4] {'seq','head'}, use_global_device_ids=true, to_apply=%region_24.25 | all-reduce | flops 11336 | bytes 90688 | tf_op jit(solution)/shard_map/psum | solution.py:346
  698.7 185.0 %all-reduce.4.cloned.1.call-done = f32[768,4888]{0,1:T(8,128)} async-done(((f32[768,4888]{0,1:T(8,128)}), f32[768,4888]{0,1:T(8,128)}) %all-reduce.4.cloned.1.call-update) | async-done | bytes 15015952
  (389 shorter events, 153.5 us)
Async XLA Ops:
  7.2 72.1 %all-gather.7.cloned.1.call-start = ((), (), s32[]{:S(2)}) async-start(), calls=%async_computation.8 | async-start | bytes 5474304 | tf_op jit(solution)/shard_map/all_gather | solution.py:82
  88.4 14.4 %all-to-all-start.2 = ((bf16[2,256,24]{1,0,2:T(2,128)(2,1)}), bf16[2,256,24]{1,0,2:T(2,128)(2,1)S(1)}, u32[]{:S(2)}, u32[]{:S(2)}) async-start(bf16[2,256,24]{1,0,2:T(2,128)(2,1)} %reshape.455), calls=%async_computation.2 | async-start | bytes 49152 | tf_op jit(solution)/shard_map/all_to_all | solution.py:94
  102.8 30.9 %all-to-all-start.1 = ((bf16[2,256,1024]{1,0,2:T(2,128)(2,1)}), bf16[2,256,1024]{1,0,2:T(2,128)(2,1)}, u32[]{:S(2)}, u32[]{:S(2)}) async-start(bf16[2,256,1024]{1,0,2:T(2,128)(2,1)} %copy.530), calls=%async_computation.1 | async-start | bytes 2097152 | tf_op jit(solution)/shard_map/all_to_all | solution.py:95
  109.1 30.4 %copy-start.92 = (f32[24]{0:T(128)S(1)}, f32[24]{0:T(128)}, u32[]{:S(2)}) copy-start(f32[24]{0:T(128)} %param.27) | copy-start | bytes 292
  109.1 30.5 %copy-start.68 = (f32[4,1792]{1,0:T(4,128)S(1)}, f32[4,1792]{1,0:T(4,128)}, u32[]{:S(2)}) copy-start(f32[4,1792]{1,0:T(4,128)} %param.25) | copy-start | bytes 86020
  109.1 30.5 %slice-start.2 = ((f32[4,1792]{1,0:T(4,128)}), f32[4,256]{1,0:T(4,128)S(1)}, s32[]{:S(2)}) async-start(f32[4,1792]{1,0:T(4,128)} %param.25), calls=%async_computation.15 | async-start | bytes 8192 | tf_op jit(solution)/shard_map/slice | solution.py:101
  109.1 30.5 %copy-start.90 = (f32[24]{0:T(128)S(1)}, f32[24]{0:T(128)}, u32[]{:S(2)}) copy-start(f32[24]{0:T(128)} %param.28) | copy-start | bytes 292
  133.6 40.9 %all-to-all-start = ((bf16[2,256,1536]{1,0,2:T(2,128)(2,1)}), bf16[2,256,1536]{1,0,2:T(2,128)(2,1)}, u32[]{:S(2)}, u32[]{:S(2)}) async-start(bf16[2,256,1536]{1,0,2:T(2,128)(2,1)} %reshape.451), calls=%async_computation | async-start | bytes 3145728 | tf_op jit(solution)/shard_map/all_to_all | solution.py:93
  138.0 96.8 %all-gather.9.cloned.1.call-start = ((), (), s32[]{:S(2)}) async-start(), calls=%async_computation.9 | async-start | bytes 1769472 | tf_op jit(solution)/shard_map/all_gather | solution.py:27
  139.6 48.2 %copy-start.49 = (f32[640]{0:T(1024)}, f32[640]{0:T(1024)S(1)}, u32[]{:S(2)}) copy-start(f32[640]{0:T(1024)S(1)} %get-tuple-element.415) | copy-start | bytes 7684
  142.5 65.3 %copy-start.2 = (f32[2,4,6,256]{2,1,3,0:T(4,128)}, f32[2,4,6,256]{2,1,3,0:T(4,128)S(1)}, u32[]{:S(2)}) copy-start(f32[2,4,6,256]{2,1,3,0:T(4,128)S(1)} %get-tuple-element.455) | copy-start | bytes 147460
  159.2 24.4 %copy-start.75 = (f32[2,1,6]{2,1,0:T(1,128)}, f32[2,1,6]{2,1,0:T(1,128)S(1)}, u32[]{:S(2)}) copy-start(f32[2,1,6]{2,1,0:T(1,128)S(1)} %get-tuple-element.483) | copy-start | bytes 148
  159.2 42.5 %copy-start.54 = (f32[2,1,6]{2,1,0:T(1,128)}, f32[2,1,6]{2,1,0:T(1,128)S(1)}, u32[]{:S(2)}) copy-start(f32[2,1,6]{2,1,0:T(1,128)S(1)} %get-tuple-element.481) | copy-start | bytes 148
  159.2 42.5 %copy-start.57 = (f32[2,1,6]{2,1,0:T(1,128)}, f32[2,1,6]{2,1,0:T(1,128)S(1)}, u32[]{:S(2)}) copy-start(f32[2,1,6]{2,1,0:T(1,128)S(1)} %get-tuple-element.482) | copy-start | bytes 148
  159.3 42.5 %copy-start.77 = (f32[2,1,6]{2,1,0:T(1,128)}, f32[2,1,6]{2,1,0:T(1,128)S(1)}, u32[]{:S(2)}) copy-start(f32[2,1,6]{2,1,0:T(1,128)S(1)} %get-tuple-element.480) | copy-start | bytes 148
  182.1 3.1 collective-permute-start
  183.7 18.1 %copy-start.72 = (f32[2,6]{1,0:T(2,128)}, f32[2,6]{1,0:T(2,128)S(1)}, u32[]{:S(2)}) copy-start(f32[2,6]{1,0:T(2,128)S(1)} %broadcast_multiply_fusion.4) | copy-start | bytes 148
  185.2 15.9 %copy-start.37 = (f32[2,4,256,6]{2,3,1,0:T(8,128)}, f32[2,4,256,6]{2,3,1,0:T(8,128)S(1)}, u32[]{:S(2)}) copy-start(f32[2,4,256,6]{2,3,1,0:T(8,128)S(1)} %copy.549) | copy-start | bytes 147460
  187.8 6.3 copy-start
  198.0 35.0 %copy-start.16 = (bf16[2,1024,128]{2,1,0:T(8,128)(2,1)}, bf16[2,1024,128]{2,1,0:T(8,128)(2,1)S(1)}, u32[]{:S(2)}) copy-start(bf16[2,1024,128]{2,1,0:T(8,128)(2,1)S(1)} %copy.535) | copy-start | bytes 1572868
  201.1 50.7 %copy-start.19 = (bf16[2,4,256,6,64]{2,1,4,3,0:T(4,128)(2,1)}, bf16[2,4,256,6,64]{2,1,4,3,0:T(4,128)(2,1)S(1)}, u32[]{:S(2)}) copy-start(bf16[2,4,256,6,64]{2,1,4,3,0:T(4,128)(2,1)S(1)} %reshape.452) | copy-start | bytes 4718596
  203.8 115.5 %all-gather.11.cloned.1.call-start = ((), (), s32[]{:S(2)}) async-start(), calls=%async_computation.10 | async-start | bytes 2433024 | tf_op jit(solution)/shard_map/all_gather | solution.py:83
  231.6 17.0 %copy-start.23 = (f32[2,1,6,64,128]{4,3,2,0,1:T(8,128)}, f32[2,1,6,64,128]{4,3,2,0,1:T(8,128)S(1)}, u32[]{:S(2)}) copy-start(f32[2,1,6,64,128]{4,3,2,0,1:T(8,128)S(1)} %get-tuple-element.451) | copy-start | bytes 1179652
  233.0 15.5 %copy-start.4 = (bf16[2,1024,128]{2,1,0:T(8,128)(2,1)}, bf16[2,1024,128]{2,1,0:T(8,128)(2,1)S(1)}, u32[]{:S(2)}) copy-start(bf16[2,1024,128]{2,1,0:T(8,128)(2,1)S(1)} %copy.534) | copy-start | bytes 1572868
  234.8 14.6 %copy-start.24 = (f32[2,1,6,64,128]{4,3,2,0,1:T(8,128)S(1)}, f32[2,1,6,64,128]{4,3,2,0,1:T(8,128)}, u32[]{:S(2)}) copy-start(f32[2,1,6,64,128]{4,3,2,0,1:T(8,128)} %get-tuple-element.452) | copy-start | bytes 1179652
  262.1 49.7 %all-to-all-start.3 = ((bf16[2,1024,384]{2,0,1:T(2,128)(2,1)}), bf16[2,1024,384]{2,0,1:T(2,128)(2,1)}, u32[]{:S(2)}, u32[]{:S(2)}) async-start(bf16[2,1024,384]{2,0,1:T(2,128)(2,1)} %copy.559), calls=%async_computation.3 | async-start | bytes 3145728 | tf_op jit(solution)/shard_map/all_to_all | solution.py:174
  319.3 8.3 copy-start.80
  319.3 8.3 copy-start.7
  319.3 8.3 copy-start.8
  319.3 8.3 copy-start.52
  330.7 6.6 copy-start.78
  333.6 41.1 %copy-start.32 = (f32[2,4,256,6]{2,3,1,0:T(8,128)S(1)}, f32[2,4,256,6]{2,3,1,0:T(8,128)}, u32[]{:S(2)}) copy-start(f32[2,4,256,6]{2,3,1,0:T(8,128)} %copy.557) | copy-start | bytes 147460
  333.6 40.9 %all-to-all-start.4 = ((bf16[2,256,1536]{1,0,2:T(2,128)(2,1)}), bf16[2,256,1536]{1,0,2:T(2,128)(2,1)S(1)}, u32[]{:S(2)}, u32[]{:S(2)}) async-start(bf16[2,256,1536]{1,0,2:T(2,128)(2,1)} %copy.569), calls=%async_computation.4 | async-start | bytes 3145728 | tf_op jit(solution)/shard_map/all_to_all | solution.py:201
  337.3 78.7 %all-gather.13.cloned.1.call-start = ((), (), s32[]{:S(2)}) async-start(), calls=%async_computation.11 | async-start | bytes 1769472 | tf_op jit(solution)/shard_map/all_gather | solution.py:27
  337.4 42.3 %copy-start.73 = (f32[2,6]{1,0:T(2,128)}, f32[2,6]{1,0:T(2,128)S(1)}, u32[]{:S(2)}) copy-start(f32[2,6]{1,0:T(2,128)S(1)} %broadcast_multiply_fusion.3) | copy-start | bytes 148
  378.0 6.0 copy-start.67
  380.8 5.1 copy-start.40
  380.8 5.1 copy-start.43
  380.8 5.1 copy-start.46
  401.4 7.4 copy-start.15
  401.4 7.5 copy-start.17
  416.0 13.9 %copy-start.51 = (f32[2,4,6]{2,0,1:T(2,128)S(1)}, f32[2,4,6]{2,0,1:T(2,128)}, u32[]{:S(2)}) copy-start(f32[2,4,6]{2,0,1:T(2,128)} %copy.553) | copy-start | bytes 580
  416.0 13.9 %copy-start.70 = (f32[2,4,6]{2,0,1:T(2,128)S(1)}, f32[2,4,6]{2,0,1:T(2,128)}, u32[]{:S(2)}) copy-start(f32[2,4,6]{2,0,1:T(2,128)} %copy.575) | copy-start | bytes 580
  445.1 22.0 %copy-start.3 = (f32[2,4,6,256]{2,1,3,0:T(4,128)S(1)}, f32[2,4,6,256]{2,1,3,0:T(4,128)}, u32[]{:S(2)}) copy-start(f32[2,4,6,256]{2,1,3,0:T(4,128)} %copy-done.2) | copy-start | bytes 147460
  445.1 22.0 %copy-start.84 = (f32[6]{0:T(128)S(1)}, f32[6]{0:T(128)}, u32[]{:S(2)}) copy-start(f32[6]{0:T(128)} %copy-done.83) | copy-start | bytes 76
  473.4 5.1 copy-start.41
  473.4 5.1 copy-start.44
  473.4 5.1 copy-start.47
  494.8 18.9 %copy-start.35 = (f32[2,4,6,256]{3,2,1,0:T(8,128)S(1)}, f32[2,4,6,256]{3,2,1,0:T(8,128)}, u32[]{:S(2)}) copy-start(f32[2,4,6,256]{3,2,1,0:T(8,128)} %copy.608) | copy-start | bytes 147460
  494.8 18.9 %copy-start.48 = (f32[2,4,6,256]{3,2,1,0:T(8,128)S(1)}, f32[2,4,6,256]{3,2,1,0:T(8,128)}, u32[]{:S(2)}) copy-start(f32[2,4,6,256]{3,2,1,0:T(8,128)} %get-tuple-element.401) | copy-start | bytes 147460
  509.8 10.0 %copy-start.50 = (f32[640]{0:T(1024)S(1)}, f32[640]{0:T(1024)}, u32[]{:S(2)}) copy-start(f32[640]{0:T(1024)} %copy-done.49) | copy-start | bytes 7684
  512.4 7.1 collective-permute-start.1
  516.3 18.4 %all-to-all-start.7 = ((bf16[4,2,1536]{2,1,0:T(2,128)(2,1)}), bf16[4,2,1536]{2,1,0:T(2,128)(2,1)S(1)}, u32[]{:S(2)}, u32[]{:S(2)}) async-start(bf16[4,2,1536]{2,1,0:T(2,128)(2,1)} %reshape.500), calls=%async_computation.7 | async-start | bytes 49152 | tf_op jit(solution)/shard_map/all_to_all | solution.py:290
  534.6 31.8 %all-to-all-start.6 = ((bf16[2,1024,256]{2,0,1:T(2,128)(2,1)}), bf16[2,1024,256]{2,0,1:T(2,128)(2,1)S(1)}, u32[]{:S(2)}, u32[]{:S(2)}) async-start(bf16[2,1024,256]{2,0,1:T(2,128)(2,1)} %copy.589), calls=%async_computation.6 | async-start | bytes 2097152 | tf_op jit(solution)/shard_map/all_to_all | solution.py:291
  542.4 28.7 %copy-start.29 = (bf16[2,256,768]{2,1,0:T(8,128)(2,1)S(1)}, bf16[2,256,768]{2,1,0:T(8,128)(2,1)}, u32[]{:S(2)}) copy-start(bf16[2,256,768]{2,1,0:T(8,128)(2,1)} %param.22) | copy-start | bytes 2359300
  542.4 28.7 %copy-start.53 = (f32[1536]{0:T(1024)S(1)}, f32[1536]{0:T(1024)}, u32[]{:S(2)}) copy-start(f32[1536]{0:T(1024)} %param.30) | copy-start | bytes 18436
  542.4 28.7 %copy-start.81 = (f32[2,256]{1,0:T(2,128)S(1)}, f32[2,256]{1,0:T(2,128)}, u32[]{:S(2)}) copy-start(f32[2,256]{1,0:T(2,128)} %copy-done.80) | copy-start | bytes 6148
  566.4 41.6 %all-to-all-start.5 = ((bf16[2,1024,384]{2,0,1:T(2,128)(2,1)}), bf16[2,1024,384]{2,0,1:T(2,128)(2,1)}, u32[]{:S(2)}, u32[]{:S(2)}) async-start(bf16[2,1024,384]{2,0,1:T(2,128)(2,1)} %copy.587), calls=%async_computation.5 | async-start | bytes 3145728 | tf_op jit(solution)/shard_map/all_to_all | solution.py:289
  570.8 312.9 %all-reduce.4.cloned.1.call-start = ((), (), s32[]{:S(2)}) async-start(), calls=%async_computation.12 | async-start | bytes 30031872
  581.3 34.5 %copy-start.33 = (bf16[2,256,256]{2,1,0:T(8,128)(2,1)}, bf16[2,256,256]{2,1,0:T(8,128)(2,1)S(1)}, u32[]{:S(2)}) copy-start(bf16[2,256,256]{2,1,0:T(8,128)(2,1)S(1)} %copy.614) | copy-start | bytes 786436
  608.1 7.7 copy-start.26
  611.9 9.0 %slice-start = ((s8[4718592]{0:T(1024)(128)(4,1)}), s8[524288]{0:T(1024)(128)(4,1)S(1)}, s32[]{:S(2)}) async-start(s8[4718592]{0:T(1024)(128)(4,1)} %bitcast.302), calls=%async_computation.13 | async-start | bytes 1048576
  615.8 5.1 slice-start.1
  648.9 48.2 %copy-start.30 = (bf16[2,256,768]{2,1,0:T(8,128)(2,1)S(1)}, bf16[2,256,768]{2,1,0:T(8,128)(2,1)}, u32[]{:S(2)}) copy-start(bf16[2,256,768]{2,1,0:T(8,128)(2,1)} %param.22) | copy-start | bytes 2359300
  (49 other events, 125.6 us)
Sparse Core Ops, SparseCore 0:
  10.9 68.3 all-gather.6
  203.9 30.0 all-gather.8
  236.8 69.6 all-gather.10
  381.9 23.6 all-gather.12
  626.8 256.8 all-reduce.3
where the time goes:
time: 908 us; the launch traced here: 897 us
  waiting for transfers between devices  399 us (44%)
  local copies, waits for them, and re-layouts  149 us (16%)
  other arithmetic  148 us (16%)
  matrix products  91.7 us (10%)
  blocking collectives  55.6 us (6%)
  starting transfers between devices  37 us (4%)
  between operations  15.4 us (2%)
    unnamed x6, waiting for transfers between devices  186 us
    all_gather x1, waiting for transfers between devices, on_device(): lax.all_gather(input_projection_weight, ('seq', 'head'), axis=0, tiled=True)  67.1 us
    another operation x8, other arithmetic  43.4 us
    psum x1, blocking collectives, on_device(): lax.psum((norm_part, kernel_full, offset_full, bias_full, decay_full, ski...  40 us
    all_to_all x1, waiting for transfers between devices, on_device(): lax.all_to_all(d_mixed_low, 'head', split_axis=2, concat_axis=1, tiled=True)  37.1 us
    all_to_all x1, waiting for transfers between devices, on_device(): lax.all_to_all(mixed_low, 'head', split_axis=1, concat_axis=2, tiled=True)  33.1 us
    all_to_all x1, waiting for transfers between devices, on_device(): lax.all_to_all(d_x_low, 'head', split_axis=1, concat_axis=2, tiled=True)  26.7 us
    all_to_all x1, waiting for transfers between devices, on_device(): lax.all_to_all(bc_tiled, 'head', split_axis=2, concat_axis=1, tiled=True)  20.9 us
  transfers between devices with their start and end apart: 15, of which 8 were waited for; matrix products, arithmetic and copies ran while one was open for 23% of the time, Pallas kernels for 0%

commit v1 on v0

v1 whole, which is shorter than its diff:
```python
import jax
import jax.numpy as jnp
from jax import lax
from jax.experimental import pallas as pl
from jax.experimental.pallas import tpu as pltpu
from jax.sharding import PartitionSpec as P

D = 768
H = 24
P_SIZE = 64
N = 128
KERNEL = 4
CH = 256
DI = H * P_SIZE
CONV = DI + 2 * N
STEP_AT = CONV
WIDE = CONV + 128
STATE = DI + 128
HALO = 16
EPSILON = 1e-05
BF = jnp.bfloat16
F32 = jnp.float32
BOTH = ("seq", "head")
PARAMS = pltpu.CompilerParams(vmem_limit_bytes=56 * 1024 * 1024)


def dot(a, b, contract=(1, 0)):
    return lax.dot_general(
        a, b, (((contract[0],), (contract[1],)), ((), ())), preferred_element_type=F32
    )


def halves(v):
    high = v.astype(BF)
    return high, (v - high.astype(F32)).astype(BF)


def head_map(rows, period=None):
    row = lax.broadcasted_iota(jnp.int32, (rows, DI), 0)
    col = lax.broadcasted_iota(jnp.int32, (rows, DI), 1)
    if period is not None:
        row = jnp.bitwise_and(row, period - 1)
    return (row == jnp.right_shift(col, 6)).astype(F32).astype(BF)


def spread_heads(v, heads):
    high, low = halves(v)
    return dot(high, heads) + dot(low, heads)


def sum_heads(v, heads):
    high, low = halves(v)
    return dot(high, heads, (1, 1)) + dot(low, heads, (1, 1))


def sigmoid(v):
    return 1.0 / (1.0 + jnp.exp(-v))


def softplus(v):
    return jnp.maximum(v, 0.0) + jnp.log1p(jnp.exp(-jnp.abs(v)))


def triangle(flip):
    row = lax.broadcasted_iota(jnp.int32, (CH, CH), 0)
    col = lax.broadcasted_iota(jnp.int32, (CH, CH), 1)
    return row <= col if flip else row >= col


def last_lanes(last):
    high = last.astype(BF).astype(F32)
    rest = last - high
    mid = rest.astype(BF).astype(F32)
    low = rest - mid
    return high + pltpu.roll(mid, 32, 1) + pltpu.roll(low, 64, 1)


def before_scan(
    hid, halo, gain, weight, taps, offset, bias, rate,
    normed_out, normed_halo_out, ext_out, pre_out, conv_out, cum_out, cumt_out,
    step_out, arg_out, state_out, ext32,
):
    def norm(v):
        v = v.astype(F32)
        scale = lax.rsqrt(jnp.mean(v * v, axis=-1, keepdims=True) + EPSILON)
        return (v * scale * gain[...]).astype(BF)

    rows = norm(hid[0])
    rows_halo = norm(halo[0])
    normed_out[0] = rows
    normed_halo_out[0] = rows_halo
    projected = dot(rows, weight[...])
    projected_halo = dot(rows_halo, weight[:, :CONV])
    low = projected[:, :CONV].astype(BF)
    low_halo = projected_halo.astype(BF)
    ext_out[0, :HALO] = low_halo
    ext_out[0, HALO:] = low
    ext32[:HALO] = low_halo.astype(F32)
    ext32[HALO:] = low.astype(F32)
    for at in range(0, CONV, 128):
        cols = slice(at, at + 128)
        pre = offset[:, cols] + taps[0:1, cols] * ext32[HALO - 3 : HALO - 3 + CH, cols]
        for k in range(1, KERNEL):
            pre = pre + taps[k : k + 1, cols] * ext32[HALO - 3 + k : HALO - 3 + k + CH, cols]
        pre_out[0, :, cols] = pre
        conv_out[0, :, cols] = (pre * sigmoid(pre)).astype(BF)
    arg = projected[:, STEP_AT:].astype(BF).astype(F32) + bias[...]
    step = softplus(arg)
    cum = jnp.dot(
        triangle(False).astype(F32),
        step * rate[...],
        precision=lax.Precision.HIGHEST,
        preferred_element_type=F32,
    )
    arg_out[0] = arg
    step_out[0] = step
    cum_out[0] = cum
    cumt_out[0] = jnp.transpose(cum)[:32]
    last = cum[CH - 1 : CH]
    heads = head_map(128)
    w = spread_heads(jnp.exp(last - cum) * step, heads)
    weighted = (conv_out[0, :, :DI].astype(F32) * w).astype(BF)
    keys = conv_out[0, :, DI : DI + N]
    state_out[0, :, :DI] = dot(keys, weighted, (0, 0)).astype(BF)
    state_out[0, :, DI:] = jnp.broadcast_to(last_lanes(last), (N, 128)).astype(BF)


def within_block(conv, cum, cumt, stept, y_out):
    keys = conv[0, :, DI : DI + N]
    queries = conv[0, :, DI + N :]
    scores = jnp.where(triangle(False), dot(queries, keys, (1, 1)), 0.0)
    half = CH // 2
    lane = lax.broadcasted_iota(jnp.int32, (half, 128), 1) < P_SIZE
    for pair in range(H // 2):
        cols = slice(pair * 128, pair * 128 + 128)
        for top, width in ((0, half), (half, CH)):
            x = conv[0, :width, cols]
            parts = []
            for h in (2 * pair, 2 * pair + 1):
                spread = cum[0, top : top + half, h : h + 1] - cumt[0, h : h + 1, :width]
                decay = jnp.exp(jnp.minimum(spread, 0.0))
                mixing = scores[top : top + half, :width] * decay * stept[0, h : h + 1, :width]
                parts.append(dot(mixing.astype(BF), x))
            y_out[0, top : top + half, cols] = jnp.where(lane, parts[0], parts[1])


def state_scan(reverse, blocks, rows, parts_in, out, decay):
    heads = head_map(128, 32)
    lane = lax.broadcasted_iota(jnp.int32, (blocks * rows, 128), 1)
    last = parts_in[:, :, DI:].reshape(blocks * rows, 128)
    last = jnp.where(lane < 96, last.astype(F32), 0.0).astype(BF)
    decay[...] = jnp.exp(dot(last, heads)).reshape(blocks, rows, DI)
    carry = jnp.zeros((rows, DI), F32)
    for k in range(blocks - 1, -1, -1) if reverse else range(blocks):
        out[k] = carry.astype(BF)
        carry = decay[k] * carry + parts_in[k, :, :DI].astype(F32)


def around_norm(
    within, conv, cum, start, gate, dmi, gain, skip,
    mixed_in_out, d_gate_out, d_y_out, dot_y_out, state_out, sums_out,
):
    heads = head_map(128)
    x = conv[0, :, :DI].astype(F32)
    queries = conv[0, :, DI + N :]
    cum_here = cum[0]
    e_cum = spread_heads(jnp.exp(cum_here), heads)
    y_scan = within[0] + dot(queries, start[0]) * e_cum
    y = (y_scan + skip[...] * x).astype(BF).astype(F32)
    gate_here = gate[0]
    sig = sigmoid(gate_here)
    act = gate_here * sig
    gated = y * act
    scale = lax.rsqrt(jnp.mean(gated * gated, axis=-1, keepdims=True) + EPSILON)
    unit = gated * scale
    mixed_in_out[0] = (unit * gain[...]).astype(BF)
    d_mixed_in = dmi[0]
    gain_part = jnp.sum(d_mixed_in * unit, axis=0, keepdims=True)
    d_unit = d_mixed_in * gain[...]
    d_gated = scale * (d_unit - unit * jnp.mean(d_unit * unit, axis=-1, keepdims=True))
    d_y_low = (d_gated * act).astype(BF)
    d_y_out[0] = d_y_low
    d_gate_out[0] = (d_gated * y * (sig * (1.0 + gate_here * (1.0 - sig)))).astype(BF)
    d_y = d_y_low.astype(F32)
    dot_y_out[0] = sum_heads(d_y * y_scan, heads)
    skip_part = jnp.sum(d_y * x, axis=0, keepdims=True)
    sums_out[0] = jnp.concatenate([gain_part, skip_part, jnp.zeros((6, DI), F32)], axis=0)
    scaled = (d_y * e_cum).astype(BF)
    state_out[0, :, :DI] = dot(queries, scaled, (0, 0)).astype(BF)
    state_out[0, :, DI:] = jnp.broadcast_to(last_lanes(cum_here[CH - 1 : CH]), (N, 128)).astype(BF)


def within_block_back(
    conv, cum, cumt, step, d_y, start, dx_out, d_keys_out, d_queries_out, scores_grad
):
    keys = conv[0, :, DI : DI + N]
    queries = conv[0, :, DI + N :]
    scores = jnp.where(triangle(True), dot(keys, queries, (1, 1)), 0.0)
    scores_grad[...] = jnp.zeros_like(scores_grad)
    half = CH // 2
    lane = lax.broadcasted_iota(jnp.int32, (half, 128), 1) < P_SIZE
    for pair in range(H // 2):
        cols = slice(pair * 128, pair * 128 + 128)
        for top, left in ((0, 0), (half, half)):
            x = conv[0, top : top + half, cols].astype(F32)
            dy = d_y[0, left:, cols]
            parts = []
            for side, h in enumerate((2 * pair, 2 * pair + 1)):
                spread = cumt[0, h : h + 1, left:] - cum[0, top : top + half, h : h + 1]
                decay = jnp.exp(jnp.minimum(spread, 0.0)) * step[0, top : top + half, h : h + 1]
                mixing = (scores[top : top + half, left:] * decay).astype(BF)
                parts.append(dot(mixing, dy))
                x_one = jnp.where(lane if side == 0 else ~lane, x, 0.0).astype(BF)
                d_mixing = dot(x_one, dy, (1, 1))
                scores_grad[top : top + half, left:] += d_mixing * decay
            dx_out[0, top : top + half, cols] = jnp.where(lane, parts[0], parts[1])
    d_scores = jnp.where(triangle(True), scores_grad[...], 0.0)
    high, low = halves(d_scores)
    d_keys_out[0] = dot(high, queries) + dot(low, queries)
    heads = head_map(128)
    scaled = (d_y[0].astype(F32) * spread_heads(jnp.exp(cum[0]), heads)).astype(BF)
    d_queries_out[0] = (
        dot(high, keys, (0, 0)) + dot(low, keys, (0, 0)) + dot(scaled, start[0], (1, 1))
    )


def after_scan(
    conv, pre, ext, cum, step, arg, d_y, dx_within, d_keys_in, d_queries, dot_y, start, after,
    skip, rate, taps,
    d_proj_out, d_halo_out, conv_sums_out, head_sums_out, d_pre, ext32,
):
    heads = head_map(128)
    x = conv[0, :, :DI].astype(F32)
    keys = conv[0, :, DI : DI + N]
    cum_here = cum[0]
    step_here = step[0]
    last = cum_here[CH - 1 : CH]
    w = spread_heads(jnp.exp(last - cum_here) * step_here, heads)
    weighted = (x * w).astype(BF)
    dx_state = dot(keys, after[0]) * w
    d_keys = d_keys_in[0] + dot(weighted, after[0], (1, 1))
    sum_within = sum_heads(x * dx_within[0], heads)
    sum_state = sum_heads(x * dx_state, heads)
    passing = jnp.sum(start[0].astype(F32) * after[0].astype(F32), axis=0, keepdims=True)
    passing = sum_heads(jnp.broadcast_to(passing, (8, DI)), heads)[0:1]
    d_last = jnp.sum(sum_state, axis=0, keepdims=True) + jnp.exp(last) * passing
    row = lax.broadcasted_iota(jnp.int32, (CH, 128), 0)
    d_cum = dot_y[0] - sum_within - sum_state + jnp.where(row == CH - 1, d_last, 0.0)
    later = jnp.dot(
        triangle(True).astype(F32),
        d_cum,
        precision=lax.Precision.HIGHEST,
        preferred_element_type=F32,
    )
    arg_here = arg[0]
    sig = sigmoid(arg_here)
    ratio = jnp.where(step_here > 1e-30, sig / jnp.maximum(step_here, 1e-30), 1.0)
    d_arg = (sum_within + sum_state) * ratio + rate[...] * later * sig
    bias_part = jnp.sum(d_arg, axis=0, keepdims=True)
    decay_part = rate[...] * jnp.sum(step_here * later, axis=0, keepdims=True)
    head_sums_out[0] = jnp.concatenate([bias_part, decay_part, jnp.zeros((6, 128), F32)], axis=0)

    dx = dx_within[0] + dx_state + skip[...] * d_y[0].astype(F32)
    ext32[...] = ext[0].astype(F32)
    d_pre[:HALO] = jnp.zeros((HALO, CONV), F32)
    d_pre[HALO + CH :] = jnp.zeros((8, CONV), F32)
    for at in range(0, CONV, 128):
        cols = slice(at, at + 128)
        v = pre[0, :, cols]
        s = sigmoid(v)
        slope = s * (1.0 + v * (1.0 - s))
        if at < DI:
            d_out = dx[:, cols]
        else:
            d_out = d_keys if at == DI else d_queries[0]
        d_here = d_out * slope
        d_pre[HALO : HALO + CH, cols] = d_here
        sums = [
            jnp.sum(
                d_here * ext32[HALO - 3 + k : HALO - 3 + k + CH, cols], axis=0, keepdims=True
            )
            for k in range(KERNEL)
        ]
        sums.append(jnp.sum(d_here, axis=0, keepdims=True))
        sums.append(jnp.zeros((3, 128), F32))
        conv_sums_out[0, :, cols] = jnp.concatenate(sums, axis=0)
        d_in = taps[0:1, cols] * d_pre[3 : 3 + HALO + CH, cols]
        for k in range(1, KERNEL):
            d_in = d_in + taps[k : k + 1, cols] * d_pre[3 - k : 3 - k + HALO + CH, cols]
        d_halo_out[0, :, cols] = d_in[:HALO].astype(BF)
        d_proj_out[0, :, cols] = d_in[HALO:].astype(BF)
    d_halo_out[0, :, STEP_AT:] = jnp.zeros((HALO, 128), BF)
    d_proj_out[0, :, STEP_AT:] = d_arg.astype(BF)


def per_sequence(body, ins, outs, scratch=(), name=None):
    seqs = next(v.shape[0] for v in ins if v.ndim == 3)

    def spec(shape):
        if len(shape) == 2:
            return pl.BlockSpec(shape, lambda s: (0, 0))
        return pl.BlockSpec((1,) + tuple(shape[1:]), lambda s: (s, 0, 0))

    return pl.pallas_call(
        body,
        grid=(seqs,),
        in_specs=[spec(v.shape) for v in ins],
        out_specs=[spec(shape) for shape, _ in outs],
        out_shape=[jax.ShapeDtypeStruct(shape, kind) for shape, kind in outs],
        scratch_shapes=list(scratch),
        compiler_params=PARAMS,
        name=name,
    )(*ins)


def scan_states(parts, groups, blocks, reverse):
    seqs = parts.shape[0]
    rows = seqs * N // blocks
    sent = lax.all_to_all(
        parts.reshape(seqs * N, STATE), BOTH, split_axis=0, concat_axis=0, tiled=True,
        axis_index_groups=groups,
    ).reshape(blocks, rows, STATE)
    if rows % 8 == 0:
        out = pl.pallas_call(
            lambda *refs: state_scan(reverse, blocks, rows, *refs),
            out_shape=jax.ShapeDtypeStruct((blocks, rows, DI), BF),
            scratch_shapes=[pltpu.VMEM((blocks, rows, DI), F32)],
            compiler_params=PARAMS,
            name="state_scan",
        )(sent)
    else:
        last = sent[:, :, DI:].astype(F32)
        last = last[..., :H] + last[..., 32 : 32 + H] + last[..., 64 : 64 + H]
        decay = jnp.repeat(jnp.exp(last), P_SIZE, axis=-1)

        def move(carry, at):
            return at[0] * carry + at[1], carry.astype(BF)

        _, out = lax.scan(
            move,
            jnp.zeros((rows, DI), F32),
            (decay, sent[:, :, :DI].astype(F32)),
            reverse=reverse,
        )
    back = lax.all_to_all(
        out.reshape(seqs * N, DI), BOTH, split_axis=0, concat_axis=0, tiled=True,
        axis_index_groups=groups,
    )
    return back.reshape(seqs, N, DI)


def pad_lanes(v, width):
    return jnp.pad(v, [(0, 0)] * (v.ndim - 1) + [(0, width - v.shape[-1])])


def gather_rows(v):
    return lax.all_gather(lax.all_gather(v, "head", axis=0, tiled=True), "seq", axis=0, tiled=True)


def scatter_rows(v):
    part = lax.psum_scatter(v, "seq", scatter_dimension=0, tiled=True)
    part = lax.psum_scatter(part, "head", scatter_dimension=0, tiled=True)
    return lax.optimization_barrier(part).astype(F32)


def on_device(
    hidden,
    out_grad,
    norm_gain,
    input_projection_weight,
    conv_weight,
    conv_bias,
    step_bias,
    decay_log,
    skip_weight,
    gate_gain,
    output_projection_weight,
):
    devices = lax.axis_size("seq") * lax.axis_size("head")
    given_rows = hidden.shape[1]
    near = CH // given_rows
    if near > 1:
        near_groups = [
            [i + j for j in range(near)] for i in range(0, lax.axis_size("head"), near)
        ]

        def to_blocks(v):
            return lax.all_to_all(
                v, "head", split_axis=0, concat_axis=1, tiled=True, axis_index_groups=near_groups
            )

        def from_blocks(v):
            return lax.all_to_all(
                v, "head", split_axis=1, concat_axis=0, tiled=True, axis_index_groups=near_groups
            )

        hidden, out_grad = to_blocks(hidden), to_blocks(out_grad)
    blocks = devices // near
    scan_groups = None
    if near > 1:
        scan_groups = [[d for d in range(devices) if d % near == r] for r in range(near)]
    seqs = hidden.shape[0]
    tokens = seqs * CH
    onward = [(i, i + near) for i in range(devices - near)]
    backward = [(i + near, i) for i in range(devices - near)]

    halo = lax.ppermute(hidden[:, CH - HALO :], BOTH, onward)
    w_gate = gather_rows(input_projection_weight[:, :DI])
    w_scan = gather_rows(pad_lanes(input_projection_weight[:, DI:], WIDE))
    w_out = gather_rows(output_projection_weight)

    gain_one = norm_gain[None]
    gain_two = gate_gain[None]
    taps = jnp.pad(conv_weight, ((0, 4), (0, 0)))
    offset = conv_bias[None]
    bias = pad_lanes(step_bias[None], 128)
    rate = pad_lanes(-jnp.exp(decay_log)[None], 128)
    skip = jnp.repeat(skip_weight, P_SIZE)[None]

    (normed, normed_halo, ext, pre, conv, cum, cumt, step, arg, parts) = per_sequence(
        before_scan,
        [hidden, halo, gain_one, w_scan, taps, offset, bias, rate],
        [
            ((seqs, CH, D), BF),
            ((seqs, HALO, D), BF),
            ((seqs, HALO + CH, CONV), BF),
            ((seqs, CH, CONV), F32),
            ((seqs, CH, CONV), BF),
            ((seqs, CH, 128), F32),
            ((seqs, 32, CH), F32),
            ((seqs, CH, 128), F32),
            ((seqs, CH, 128), F32),
            ((seqs, N, STATE), BF),
        ],
        [pltpu.VMEM((HALO + CH, CONV), F32)],
        name="before_scan",
    )
    starts = scan_states(parts, scan_groups, blocks, False)

    stept = jnp.swapaxes(step, 1, 2)[:, :32]
    (within,) = per_sequence(
        within_block, [conv, cum, cumt, stept], [((seqs, CH, DI), F32)], name="within_block"
    )
    normed_rows = normed.reshape(tokens, D)
    gate = jnp.dot(normed_rows, w_gate, preferred_element_type=F32).reshape(seqs, CH, DI)
    cotangent = out_grad.reshape(tokens, D)
    d_mixed_in = jnp.dot(cotangent, w_out, preferred_element_type=F32).reshape(seqs, CH, DI)

    mixed_in, d_gate, d_y, dot_y, parts_back, row_sums = per_sequence(
        around_norm,
        [within, conv, cum, starts, gate, d_mixed_in, gain_two, skip],
        [
            ((seqs, CH, DI), BF),
            ((seqs, CH, DI), BF),
            ((seqs, CH, DI), BF),
            ((seqs, CH, 128), F32),
            ((seqs, N, STATE), BF),
            ((seqs, 8, DI), F32),
        ],
        name="around_norm",
    )
    afters = scan_states(parts_back, scan_groups, blocks, True)

    mixed_rows = mixed_in.reshape(tokens, DI)
    branch = dot(mixed_rows, w_out, (1, 1)).reshape(seqs, CH, D)
    widened = hidden.astype(F32)
    mixed = (widened + branch).astype(BF)
    d_gate_rows = d_gate.reshape(tokens, DI)
    out_rows = scatter_rows(dot(cotangent, mixed_rows, (0, 0)).astype(BF))
    gate_rows = scatter_rows(dot(normed_rows, d_gate_rows, (0, 0)).astype(BF))

    dx_within, d_keys, d_queries = per_sequence(
        within_block_back,
        [conv, cum, cumt, step, d_y, starts],
        [((seqs, CH, DI), F32), ((seqs, CH, N), F32), ((seqs, CH, N), F32)],
        [pltpu.VMEM((CH, CH), F32)],
        name="within_block_back",
    )
    d_scan, d_halo, conv_sums, head_sums = per_sequence(
        after_scan,
        [
            conv, pre, ext, cum, step, arg, d_y, dx_within, d_keys, d_queries, dot_y, starts,
            afters, skip, rate, taps,
        ],
        [
            ((seqs, CH, WIDE), BF),
            ((seqs, HALO, WIDE), BF),
            ((seqs, 8, CONV), F32),
            ((seqs, 8, 128), F32),
        ],
        [pltpu.VMEM((HALO + CH + 8, CONV), F32), pltpu.VMEM((HALO + CH, CONV), F32)],
        name="after_scan",
    )
    d_scan_rows = d_scan.reshape(tokens, WIDE)
    d_halo_rows = d_halo.reshape(seqs * HALO, WIDE)
    scan_term = dot(normed_rows, d_scan_rows, (0, 0)) + dot(
        normed_halo.reshape(seqs * HALO, D), d_halo_rows, (0, 0)
    )
    scan_rows = scatter_rows(scan_term.astype(BF))

    d_normed_halo = dot(d_halo_rows, w_scan, (1, 1)).reshape(seqs, HALO, D)
    from_next = lax.ppermute(d_normed_halo[:, HALO - 8 :], BOTH, backward)
    d_normed = (dot(d_gate_rows, w_gate, (1, 1)) + dot(d_scan_rows, w_scan, (1, 1))).reshape(
        seqs, CH, D
    )
    d_normed = d_normed + jnp.pad(from_next, ((0, 0), (CH - 8, 0), (0, 0)))
    scale_one = lax.rsqrt(jnp.mean(widened * widened, axis=-1, keepdims=True) + EPSILON)
    unit_one = widened * scale_one
    norm_part = jnp.sum(d_normed * unit_one, axis=(0, 1))
    d_unit_one = d_normed * norm_gain
    hidden_grad = out_grad.astype(F32) + scale_one * (
        d_unit_one - unit_one * jnp.mean(d_unit_one * unit_one, axis=-1, keepdims=True)
    )
    if near > 1:
        mixed, hidden_grad = from_blocks(mixed), from_blocks(hidden_grad)

    row_sums = jnp.sum(row_sums, axis=0)
    conv_sums = jnp.sum(conv_sums, axis=0)
    head_sums = jnp.sum(head_sums, axis=0)
    pieces = (
        norm_part,
        conv_sums[:KERNEL].reshape(-1),
        conv_sums[KERNEL],
        head_sums[0, :H],
        head_sums[1, :H],
        jnp.sum(row_sums[1].reshape(H, P_SIZE), axis=1),
        row_sums[0],
    )
    summed = lax.psum(jnp.concatenate(pieces), BOTH)
    outs, at = [], 0
    for piece in pieces:
        outs.append(summed[at : at + piece.shape[0]])
        at += piece.shape[0]
    in_rows = jnp.concatenate([gate_rows, scan_rows[:, : CONV + H]], axis=1)
    return (
        mixed,
        hidden_grad,
        outs[0],
        in_rows,
        outs[1].reshape(KERNEL, CONV),
        outs[2],
        outs[3],
        outs[4],
        outs[5],
        outs[6],
        out_rows,
    )


def solution(mesh):
    rows = P(None, BOTH, None)
    weight = P(BOTH, None)
    return jax.shard_map(
        on_device,
        mesh=mesh,
        in_specs=(rows, rows, P(), weight, P(), P(), P(), P(), P(), P(), weight),
        out_specs=(rows, rows, P(), weight, P(), P(), P(), P(), P(), P(), weight),
        check_vma=False,
    )
```

time: 908 us -> 369 us (0.41); the launches traced: 897 us -> 368 us
  waiting for transfers between devices: 399 us -> 98.6 us
  other arithmetic: 148 us -> 4.2 us
  local copies, waits for them, and re-layouts: 149 us -> 18.6 us
  blocking collectives: 55.6 us -> 117 us
  Pallas kernels: 0 us -> 59.8 us
  matrix products: 91.7 us -> 38 us
  starting transfers between devices: 37 us -> 17.6 us
    unnamed x6 -> x12, waiting for transfers between devices: 186 us -> 41.1 us
    all_to_all x8 -> x3, waiting for transfers between devices: 146 us -> 26.6 us  [the longest x1 16.4 us: scan_states(): lax.all_to_all(parts.reshape(seqs * N, STATE), BOTH, split_axis=0, concat...]
    pallas_call x0 -> x7, Pallas kernels: none -> 59.8 us  [the longest x5 54.7 us: per_sequence(): pl.pallas_call(body, grid=(seqs,), in_specs=[spec(v.shape) for v in ins],...]
    all_gather x4 -> x3, waiting for transfers between devices: 67.1 us -> 10.5 us  [gather_rows(): lax.all_gather(lax.all_gather(v, 'head', axis=0, tiled=True), 'seq', axis...]
    dot_general x18 -> x10, matrix products: 91.7 us -> 38 us  [the longest x8 28.5 us: dot(): lax.dot_general(a, b, (((contract[0],), (contract[1],)), ((), ())), prefe...]
    another operation x10 -> x0, other arithmetic: 43.5 us -> none
    all_gather x1 -> x3, blocking collectives: 15.5 us -> 48.5 us  [gather_rows(): lax.all_gather(v, 'head', axis=0, tiled=True)]
    convert_element_type x24 -> x0, other arithmetic: 30.3 us -> none  [the longest x16 10.3 us: step(): part[at].astype(own.dtype)]
  transfers between devices with their start and end apart: 15 -> 14, of which waited for: 8 -> 8; matrix products, arithmetic and copies ran while one was open for 23% -> 13% of each run, Pallas kernels for 0% -> 13%
where the time goes in v1:
time: 369 us; the launch traced here: 368 us
  blocking collectives  117 us (32%)
  waiting for transfers between devices  98.6 us (27%)
  Pallas kernels  59.8 us (16%)
  matrix products  38 us (10%)
  local copies, waits for them, and re-layouts  18.6 us (5%)
  starting transfers between devices  17.6 us (5%)
  between operations  14.2 us (4%)
  other arithmetic  4.2 us (1%)
    pallas_call x5, Pallas kernels, per_sequence(): pl.pallas_call(body, grid=(seqs,), in_specs=[spec(v.shape) for v in ins],...  54.7 us
    all_gather x3, blocking collectives, gather_rows(): lax.all_gather(v, 'head', axis=0, tiled=True)  48.5 us
    psum x1, blocking collectives, on_device(): summed = lax.psum(jnp.concatenate(pieces), BOTH)  41.5 us
    unnamed x12, waiting for transfers between devices  41.1 us
    dot_general x8, matrix products, dot(): lax.dot_general(a, b, (((contract[0],), (contract[1],)), ((), ())), prefe...  28.5 us
    all_to_all x1, blocking collectives, scan_states(): lax.all_to_all(parts.reshape(seqs * N, STATE), BOTH, split_axis=0, concat...  27 us
    reduce_scatter x1, waiting for transfers between devices, scatter_rows(): part = lax.psum_scatter(part, 'head', scatter_dimension=0, tiled=True)  18.5 us
    all_to_all x1, waiting for transfers between devices, scan_states(): lax.all_to_all(parts.reshape(seqs * N, STATE), BOTH, split_axis=0, concat...  16.4 us
  transfers between devices with their start and end apart: 14, of which 8 were waited for; matrix products, arithmetic and copies ran while one was open for 13% of the time, Pallas kernels for 13%

profile of v1, /device:TPU:0, one launch (start us, length us, event | category | flops | bytes accessed | tf_op | source)
XLA Modules:
  0.0 368.1 jit_solution(7212405115827950307)
XLA Ops:
  7.3 0.9 slice.59
  8.2 16.7 %all_gather.18 = bf16[96,1920]{1,0:T(8,128)(2,1)} all-gather(bf16[24,1920]{1,0:T(8,128)(2,1)S(1)} %pad.19), channel_id=1, replica_groups=mesh['seq'=8,'head'=4] {'head'}, dimensions={0}, use_global_device_ids=true | all-gather | bytes 460800 | tf_op jit(solution)/shard_map/all_gather | solution.py:357
  25.0 17.2 %all_gather.22 = bf16[96,1536]{1,0:T(8,128)(2,1)} all-gather(bf16[24,1536]{1,0:T(8,128)(2,1)} %param.21), channel_id=1, replica_groups=mesh['seq'=8,'head'=4] {'head'}, dimensions={0}, use_global_device_ids=true | all-gather | bytes 368640 | tf_op jit(solution)/shard_map/all_gather | solution.py:357
  42.3 14.6 %all_gather.20 = bf16[96,1536]{1,0:T(8,128)(2,1)} all-gather(bf16[24,1536]{1,0:T(8,128)(2,1)S(1)} %slice-done), channel_id=1, replica_groups=mesh['seq'=8,'head'=4] {'head'}, dimensions={0}, use_global_device_ids=true | all-gather | bytes 368640 | tf_op jit(solution)/shard_map/all_gather | solution.py:357
  56.9 0.8 slice.58
  57.7 2.3 collective-permute-start
  60.1 0.6 pad.20.taps
  60.7 0.5 pad.22.rate
  61.2 0.6 broadcast_in_dim.20.offset
  61.8 0.6 broadcast_in_dim.19.gain
  62.4 0.5 pad.21.bias
  62.9 0.6 copy-done.12
  63.5 11.7 %before_scan.1 = (bf16[2,256,768]{2,1,0:T(8,128)(2,1)}, bf16[2,16,768]{2,1,0:T(8,128)(2,1)}, bf16[2,272,1792]{2,1,0:T(8,128)(2,1)}, f32[2,256,1792]{2,1,0:T(8,12...) custom-call(bf16[2,256,768]{2,1,0:T(8,128)(2,1)} %hid.1, ...), custom_call_target="tpu_custom_call" | custom-call | tf_op jit(solution)/shard_map/before_scan/pallas_call | solution.py:304
  75.2 27.0 %all_to_all.30.refs_0_ = bf16[32,8,1664]{2,1,0:T(8,128)(2,1)} all-to-all(bf16[32,8,1664]{2,1,0:T(8,128)(2,1)} %bitcast.69), channel_id=1, replica_groups=mesh['seq'=8,'head'=4] {'seq','head'}, dimensions={0} | all-to-all | bytes 1703936 | tf_op jit(solution)/shard_map/all_to_all | solution.py:319
  102.2 2.5 state_scan.2
  104.7 4.4 %all-to-all-start.1 = ((bf16[32,8,1536]{2,1,0:T(8,128)(2,1)}), bf16[32,8,1536]{2,1,0:T(8,128)(2,1)S(1)}, u32[]{:S(2)}, u32[]{:S(2)}) async-start(bf16[32,8,1536]{2,1,0:T(8,128)(2,1)} %state_scan.2), calls=%async_computation.1 | async-start | bytes 1572864 | tf_op jit(solution)/shard_map/all_to_all | solution.py:345
  109.4 0.7 broadcast_in_dim_reshape.3.skip
  110.1 0.6 broadcast_in_dim.22.gain
  110.7 4.8 %fusion.6.dmi = f32[2,256,1536]{2,1,0:T(8,128)} fusion(bf16[2,256,768]{2,1,0:T(8,128)(2,1)S(1)} %copy-done.5, bf16[768,1536]{1,0:T(8,128)(2,1)} %all-gather.8.cloned.1.call-done), kind=kOutput, calls=%fused_computation.12 | convolution fusion | flops 1207959552 | bytes 6291456 | tf_op jit(solution)/shard_map/dot_general | solution.py:447
  115.6 0.6 slice.78.stept
  116.2 5.4 %within_block.1.within = f32[2,256,1536]{2,1,0:T(8,128)} custom-call(bf16[2,256,1792]{2,1,0:T(8,128)(2,1)} %get-tuple-element.34.conv, f32[2,256,128]{2,1,0:T(8,128)} %get-tuple-element.35.cum, f32[2,32,256]{2,1,0:T(8,128)} %get-tuple-element.36.cumt, f32[2,32,256]{2,1,0:T(8,128)} %slice.78.stept), custom_call_target="tpu_custom_call" | custom-call | tf_op jit(solution)/shard_map/within_block/pallas_call | solution.py:304
  121.7 10.5 %all-gather.6.cloned.1.call-done = bf16[768,1536]{1,0:T(8,128)(2,1)} async-done(((bf16[96,1536]{1,0:T(8,128)(2,1)}), bf16[768,1536]{1,0:T(8,128)(2,1)}) %all-gather.6.cloned.1.call-update) | async-done | bytes 2359312 | tf_op jit(solution)/shard_map/all_gather | solution.py:357
  132.2 4.8 %fusion.8.gate = f32[2,256,1536]{2,1,0:T(8,128)} fusion(bf16[2,256,768]{2,1,0:T(8,128)(2,1)S(1)} %copy-done.6, bf16[768,1536]{1,0:T(8,128)(2,1)} %all-gather.6.cloned.1.call-done), kind=kOutput, calls=%fused_computation.14 | convolution fusion | flops 1207959552 | bytes 6291456 | tf_op jit(solution)/shard_map/dot_general | solution.py:445
  137.0 0.9 copy-done.1
  137.9 11.2 %around_norm.1 = (bf16[2,256,1536]{2,1,0:T(8,128)(2,1)}, bf16[2,256,1536]{2,1,0:T(8,128)(2,1)}, bf16[2,256,1536]{2,1,0:T(8,128)(2,1)}, f32[2,256,128]{2,1,0:T(8,...) custom-call(f32[2,256,1536]{2,1,0:T(8,128)} %within_block.1.within, ...), custom_call_target="tpu_custom_call" | custom-call | tf_op jit(solution)/shard_map/around_norm/pallas_call | solution.py:304
  149.1 2.8 fusion.1
  151.9 2.5 copy.40
  154.4 4.1 %all-to-all-start.2 = ((bf16[32,8,1664]{2,1,0:T(8,128)(2,1)}), bf16[32,8,1664]{2,1,0:T(8,128)(2,1)S(1)}, u32[]{:S(2)}, u32[]{:S(2)}) async-start(bf16[32,8,1664]{2,1,0:T(8,128)(2,1)} %bitcast.8), calls=%async_computation.2 | async-start | bytes 1703936 | tf_op jit(solution)/shard_map/all_to_all | solution.py:319
  158.5 4.4 %bitcast_convert_fusion.1 = bf16[768,1536]{1,0:T(8,128)(2,1)} fusion(bf16[2,256,768]{2,1,0:T(8,128)(2,1)S(1)} %copy-done.7, bf16[2,256,1536]{2,1,0:T(8,128)(2,1)} %get-tuple-element.41), kind=kOutput, calls=%fused_computation.3 | convolution fusion | flops 1209139200 | bytes 4718592 | tf_op jit(solution)/shard_map/dot_general | solution.py:28
  163.0 16.4 %all-to-all-done.2.refs_0_ = bf16[32,8,1664]{2,1,0:T(8,128)(2,1)S(1)} async-done(((bf16[32,8,1664]{2,1,0:T(8,128)(2,1)}), bf16[32,8,1664]{2,1,0:T(8,128)(2,1)S(1)}, u32[]{:S(2)}, u32[]{:S(2)}) %all-to-all-start.2) | async-done | bytes 852000 | tf_op jit(solution)/shard_map/all_to_all | solution.py:319
  179.5 0.9 copy-done.2
  180.4 2.6 state_scan.3
  182.9 4.5 %all-to-all-start.3 = ((bf16[32,8,1536]{2,1,0:T(8,128)(2,1)}), bf16[32,8,1536]{2,1,0:T(8,128)(2,1)S(1)}, u32[]{:S(2)}, u32[]{:S(2)}) async-start(bf16[32,8,1536]{2,1,0:T(8,128)(2,1)} %state_scan.3), calls=%async_computation.3 | async-start | bytes 1572864 | tf_op jit(solution)/shard_map/all_to_all | solution.py:345
  187.4 0.3 reduce-scatter.17.cloned.1.call-start
  187.7 9.2 %within_block_back.1 = (f32[2,256,1536]{2,1,0:T(8,128)}, f32[2,256,128]{2,1,0:T(8,128)}, f32[2,256,128]{2,1,0:T(8,128)}) custom-call(bf16[2,256,1792]{2,1,0:T(8,128)(2,1)} %get-tuple-element.34.conv, f32[2,256,128]{2,1,0:T(8,128)} %get-tuple-element.35.cum, f32[2,32,256]{2,1,0:T(8,128)} %get-tuple-element.36.cumt, f32[2,256,128]{2,1,0:T(8,128)} %get-tuple-element.37.step, ...), custom_call_target="tpu_custom_call" | custom-call | tf_op jit(solution)/shard_map/within_block_back/pallas_call | solution.py:304
  196.9 10.2 %all-to-all-done.3 = bf16[32,8,1536]{2,1,0:T(8,128)(2,1)S(1)} async-done(((bf16[32,8,1536]{2,1,0:T(8,128)(2,1)}), bf16[32,8,1536]{2,1,0:T(8,128)(2,1)S(1)}, u32[]{:S(2)}, u32[]{:S(2)}) %all-to-all-start.3) | async-done | bytes 786464 | tf_op jit(solution)/shard_map/all_to_all | solution.py:345
  207.1 0.9 copy-done.3
  207.9 17.3 %after_scan.1 = (bf16[2,256,1920]{2,1,0:T(8,128)(2,1)}, bf16[2,16,1920]{2,1,0:T(8,128)(2,1)}, f32[2,8,1792]{2,1,0:T(8,128)}, f32[2,8,128]{2,1,0:T(8,128)}) custom-call(bf16[2,256,1792]{2,1,0:T(8,128)(2,1)} %get-tuple-element.34.conv, f32[2,256,1792]{2,1,0:T(8,128)} %get-tuple-element.42.pre, bf16[2,272,1792]{2,1,0:T(8,128)(2,1)} %get-tuple-element.43.ext, ...), custom_call_target="tpu_custom_call" | custom-call | tf_op jit(solution)/shard_map/after_scan/pallas_call | solution.py:304
  225.3 3.8 %fusion.25 = f32[768,1920,1]{1,0,2:T(8,128)S(1)} fusion(bf16[2,256,768]{2,1,0:T(8,128)(2,1)S(1)} %copy-done.7, bf16[2,256,1920]{2,1,0:T(8,128)(2,1)} %get-tuple-element.51), kind=kOutput, calls=%fused_computation.40 | convolution fusion | flops 1509949440 | bytes 8650752 | tf_op jit(solution)/shard_map/dot_general | solution.py:28
  229.1 2.6 fusion
  231.7 0.3 reduce-scatter.21.cloned.1.call-start
  232.0 0.8 copy-done
  232.8 0.2 fusion.19
  233.3 5.0 %fusion.24 = f32[512,768]{1,0:T(8,128)} fusion(bf16[512,1536]{1,0:T(8,128)(2,1)} %bitcast.72, bf16[768,1536]{1,0:T(8,128)(2,1)} %all-gather.6.cloned.1.call-done), kind=kOutput, calls=%fused_computation.39 | convolution fusion | flops 1207959552 | bytes 5505024 | tf_op jit(solution)/shard_map/dot_general | solution.py:28
  238.3 2.3 fusion.18
  240.7 2.8 fusion.2
  243.5 1.3 collective-permute-start.1
  244.8 4.8 %convolution_add_fusion = f32[512,768]{1,0:T(8,128)S(1)} fusion(f32[512,768]{1,0:T(8,128)} %fusion.24, bf16[512,1920]{1,0:T(8,128)(2,1)} %bitcast.68, bf16[768,1920]{1,0:T(8,128)(2,1)} %all-gather.4.cloned.1.call-done.weight), kind=kOutput, calls=%fused_computation.27 | convolution fusion | flops 1510342656 | bytes 8060928 | tf_op jit(solution)/shard_map/dot_general | solution.py:28
  249.8 0.4 collective-permute-done.1
  250.2 0.5 fusion.17
  250.8 41.5 %psum.7 = f32[11336]{0:T(1024)S(1)} all-reduce(f32[11336]{0:T(1024)S(1)} %concatenate.9), channel_id=1, replica_groups=mesh['seq'=8,'head'=4] {'seq','head'}, use_global_device_ids=true, to_apply=%region_7.8 | all-reduce | flops 11336 | bytes 90688 | tf_op jit(solution)/shard_map/psum | solution.py:529
  292.3 0.6 slice.86
  292.9 0.7 slice.90
  293.6 0.6 slice.83
  294.2 0.6 reshape.102
  294.8 1.5 reduce-scatter.17.cloned.1.call-done
  296.3 0.6 fusion.23
  296.9 1.6 fusion.16
  298.5 20.0 %reduce-scatter.21.cloned.1.call-done = bf16[24,1536]{1,0:T(8,128)(2,1)} async-done(((bf16[96,1536]{1,0:T(8,128)(2,1)}), bf16[24,1536]{1,0:T(8,128)(2,1)}) %reduce-scatter.21.cloned.1.call-update) | async-done | bytes 73744
  318.5 1.1 copy.43
  319.6 0.8 copy.36
  320.4 18.5 %reduce-scatter.15.cloned.1.call-done = bf16[24,1536]{1,0:T(8,128)(2,1)} async-done(((bf16[96,1536]{1,0:T(8,128)(2,1)}), bf16[24,1536]{1,0:T(8,128)(2,1)}) %reduce-scatter.15.cloned.1.call-update) | async-done | bytes 73744 | tf_op jit(solution)/shard_map/reduce_scatter | solution.py:362
  338.9 20.9 %reduce-scatter.23.cloned.1.call-done = bf16[24,1920]{1,0:T(8,128)(2,1)} async-done(((bf16[96,1920]{1,0:T(8,128)(2,1)}), bf16[24,1920]{1,0:T(8,128)(2,1)}) %reduce-scatter.23.cloned.1.call-update) | async-done | bytes 92176
  359.8 1.7 maximum_convert_fusion
  (83 shorter events, 1.3 us)
Async XLA Ops:
  7.2 35.1 %slice-start = ((bf16[24,3352]{1,0:T(8,128)(2,1)}), bf16[24,1536]{1,0:T(8,128)(2,1)S(1)}, s32[]{:S(2)}) async-start(bf16[24,3352]{1,0:T(8,128)(2,1)} %param.14), calls=%async_computation.19 | async-start | bytes 147456 | tf_op jit(solution)/shard_map/slice | solution.py:408
  7.2 52.9 %copy-start.21 = (f32[24]{0:T(128)S(1)}, f32[24]{0:T(128)}, u32[]{:S(2)}) copy-start(f32[24]{0:T(128)} %param.18) | copy-start | bytes 292
  7.2 52.9 %copy-start.14 = (f32[4,1792]{1,0:T(4,128)S(1)}, f32[4,1792]{1,0:T(4,128)}, u32[]{:S(2)}) copy-start(f32[4,1792]{1,0:T(4,128)} %param.15) | copy-start | bytes 86020
  7.2 54.0 %copy-start.17 = (f32[1792]{0:T(1024)S(1)}, f32[1792]{0:T(1024)}, u32[]{:S(2)}) copy-start(f32[1792]{0:T(1024)} %param.16) | copy-start | bytes 21508
  7.2 54.6 %copy-start.13 = (f32[768]{0:T(1024)S(1)}, f32[768]{0:T(1024)}, u32[]{:S(2)}) copy-start(f32[768]{0:T(1024)} %param.13) | copy-start | bytes 9220
  7.2 55.2 %copy-start.22 = (f32[24]{0:T(128)S(1)}, f32[24]{0:T(128)}, u32[]{:S(2)}) copy-start(f32[24]{0:T(128)} %param.17) | copy-start | bytes 292
  7.2 55.7 %all-gather.4.cloned.1.call-start = ((), (), s32[]{:S(2)}) async-start(), calls=%async_computation.10 | async-start | bytes 3317760 | tf_op jit(solution)/shard_map/all_gather | solution.py:357
  24.9 85.8 %all-gather.8.cloned.1.call-start = ((), (), s32[]{:S(2)}) async-start(), calls=%async_computation.12 | async-start | bytes 2654208 | tf_op jit(solution)/shard_map/all_gather | solution.py:357
  42.2 90.0 %all-gather.6.cloned.1.call-start = ((), (), s32[]{:S(2)}) async-start(), calls=%async_computation.11 | async-start | bytes 2654208 | tf_op jit(solution)/shard_map/all_gather | solution.py:357
  57.7 5.2 %collective-permute-start = (bf16[2,16,768]{2,1,0:T(8,128)(2,1)S(1)}, bf16[2,16,768]{2,1,0:T(8,128)(2,1)S(1)}, u32[]{:S(2)}, u32[]{:S(2)}) collective-permute-start(bf16[2,16,768]{2,1,0:T(8,128)(2,1)S(1)} %slice.58), channel_id=1, source_target_pairs={{0,1},{1,2},{2,3},{3,4},{4,5},{5,6},{6,7},{7,8},{8,9},{9,10},{10,1... | collective-permute-start | bytes 147464 | tf_op jit(solution)/shard_map/ppermute | solution.py:407
  62.9 0.6 copy-start.12
  102.2 7.2 %copy-start.18 = (f32[24]{0:T(128)S(1)}, f32[24]{0:T(128)}, u32[]{:S(2)}) copy-start(f32[24]{0:T(128)} %param.19) | copy-start | bytes 292
  102.2 7.9 %copy-start.15 = (f32[1536]{0:T(1024)S(1)}, f32[1536]{0:T(1024)}, u32[]{:S(2)}) copy-start(f32[1536]{0:T(1024)} %param.20) | copy-start | bytes 18436
  102.2 8.5 %copy-start.5 = (bf16[2,256,768]{2,1,0:T(8,128)(2,1)S(1)}, bf16[2,256,768]{2,1,0:T(8,128)(2,1)}, u32[]{:S(2)}) copy-start(bf16[2,256,768]{2,1,0:T(8,128)(2,1)} %param.12) | copy-start | bytes 2359300
  104.7 32.3 %all-to-all-start.1 = ((bf16[32,8,1536]{2,1,0:T(8,128)(2,1)}), bf16[32,8,1536]{2,1,0:T(8,128)(2,1)S(1)}, u32[]{:S(2)}, u32[]{:S(2)}) async-start(bf16[32,8,1536]{2,1,0:T(8,128)(2,1)} %state_scan.2), calls=%async_computation.1 | async-start | bytes 1572864 | tf_op jit(solution)/shard_map/all_to_all | solution.py:345
  109.1 131.5 %reduce-scatter.19.cloned.1.call-start = ((), (), s32[]{:S(2)}) async-start(), calls=%async_computation.16 | async-start | bytes 2654208
  110.7 4.8 %copy-start.4 = (f32[2,256,128]{2,1,0:T(8,128)S(1)}, f32[2,256,128]{2,1,0:T(8,128)}, u32[]{:S(2)}) copy-start(f32[2,256,128]{2,1,0:T(8,128)} %get-tuple-element.37.step) | copy-start | bytes 786436
  116.2 15.9 %copy-start.6 = (bf16[2,256,768]{2,1,0:T(8,128)(2,1)S(1)}, bf16[2,256,768]{2,1,0:T(8,128)(2,1)}, u32[]{:S(2)}) copy-start(bf16[2,256,768]{2,1,0:T(8,128)(2,1)} %get-tuple-element.39) | copy-start | bytes 2359300
  137.0 0.9 copy-start.1
  154.4 4.2 %copy-start.7 = (bf16[2,256,768]{2,1,0:T(8,128)(2,1)S(1)}, bf16[2,256,768]{2,1,0:T(8,128)(2,1)}, u32[]{:S(2)}) copy-start(bf16[2,256,768]{2,1,0:T(8,128)(2,1)} %get-tuple-element.39) | copy-start | bytes 2359300
  154.4 25.1 %all-to-all-start.2 = ((bf16[32,8,1664]{2,1,0:T(8,128)(2,1)}), bf16[32,8,1664]{2,1,0:T(8,128)(2,1)S(1)}, u32[]{:S(2)}, u32[]{:S(2)}) async-start(bf16[32,8,1664]{2,1,0:T(8,128)(2,1)} %bitcast.8), calls=%async_computation.2 | async-start | bytes 1703936 | tf_op jit(solution)/shard_map/all_to_all | solution.py:319
  158.5 91.2 %reduce-scatter.13.cloned.1.call-start = ((), (), s32[]{:S(2)}) async-start(), calls=%async_computation.13 | async-start | bytes 2654208 | tf_op jit(solution)/shard_map/reduce_scatter | solution.py:361
  179.5 0.9 copy-start.2
  182.9 24.1 %all-to-all-start.3 = ((bf16[32,8,1536]{2,1,0:T(8,128)(2,1)}), bf16[32,8,1536]{2,1,0:T(8,128)(2,1)S(1)}, u32[]{:S(2)}, u32[]{:S(2)}) async-start(bf16[32,8,1536]{2,1,0:T(8,128)(2,1)} %state_scan.3), calls=%async_computation.3 | async-start | bytes 1572864 | tf_op jit(solution)/shard_map/all_to_all | solution.py:345
  187.4 108.8 %reduce-scatter.17.cloned.1.call-start = ((), (), s32[]{:S(2)}) async-start(), calls=%async_computation.15 | async-start | bytes 3317760 | tf_op jit(solution)/shard_map/reduce_scatter | solution.py:361
  207.1 0.9 copy-start.3
  225.3 3.8 %copy-start.8 = (bf16[2,16,1920]{2,1,0:T(8,128)(2,1)S(1)}, bf16[2,16,1920]{2,1,0:T(8,128)(2,1)}, u32[]{:S(2)}) copy-start(bf16[2,16,1920]{2,1,0:T(8,128)(2,1)} %get-tuple-element.52) | copy-start | bytes 368644
  225.3 3.8 %copy-start.11 = (bf16[2,16,768]{2,1,0:T(8,128)(2,1)S(1)}, bf16[2,16,768]{2,1,0:T(8,128)(2,1)}, u32[]{:S(2)}) copy-start(bf16[2,16,768]{2,1,0:T(8,128)(2,1)} %get-tuple-element.56) | copy-start | bytes 147460
  231.6 1.1 copy-start
  231.6 1.4 copy-start.10
  231.7 86.8 %reduce-scatter.21.cloned.1.call-start = ((), (), s32[]{:S(2)}) async-start(), calls=%async_computation.17 | async-start | bytes 368640
  233.3 5.0 %copy-start.19 = (bf16[768,1536]{1,0:T(8,128)(2,1)S(1)}, bf16[768,1536]{1,0:T(8,128)(2,1)}, u32[]{:S(2)}) copy-start(bf16[768,1536]{1,0:T(8,128)(2,1)} %all-gather.8.cloned.1.call-done) | copy-start | bytes 7077892
  233.3 5.0 %copy-start.20 = (bf16[2,256,1536]{2,1,0:T(8,128)(2,1)S(1)}, bf16[2,256,1536]{2,1,0:T(8,128)(2,1)}, u32[]{:S(2)}) copy-start(bf16[2,256,1536]{2,1,0:T(8,128)(2,1)} %get-tuple-element.40) | copy-start | bytes 4718596
  240.6 4.2 %copy-start.9 = (f32[2,8,1792]{2,1,0:T(8,128)S(1)}, f32[2,8,1792]{2,1,0:T(8,128)}, u32[]{:S(2)}) copy-start(f32[2,8,1792]{2,1,0:T(8,128)} %get-tuple-element.53) | copy-start | bytes 344068
  240.6 4.2 %copy-start.16 = (f32[2,8,128]{2,1,0:T(8,128)S(1)}, f32[2,8,128]{2,1,0:T(8,128)}, u32[]{:S(2)}) copy-start(f32[2,8,128]{2,1,0:T(8,128)} %get-tuple-element.54) | copy-start | bytes 24580
  240.6 98.3 %reduce-scatter.15.cloned.1.call-start = ((), (), s32[]{:S(2)}) async-start(), calls=%async_computation.14 | async-start | bytes 368640 | tf_op jit(solution)/shard_map/reduce_scatter | solution.py:362
  243.5 6.7 %collective-permute-start.1 = (f32[2,8,768]{2,1,0:T(8,128)S(1)}, f32[2,8,768]{2,1,0:T(8,128)S(1)}, u32[]{:S(2)}, u32[]{:S(2)}) collective-permute-start(f32[2,8,768]{2,1,0:T(8,128)S(1)} %fusion.2), channel_id=1, source_target_pairs={{1,0},{2,1},{3,2},{4,3},{5,4},{6,5},{7,6},{8,7},{9,8},{10,9},{11,1... | collective-permute-start | bytes 147464 | tf_op jit(solution)/shard_map/ppermute | solution.py:502
  249.7 110.2 %reduce-scatter.23.cloned.1.call-start = ((), (), s32[]{:S(2)}) async-start(), calls=%async_computation.18 | async-start | bytes 460800
Sparse Core Ops, SparseCore 0:
  25.0 33.3 all-gather.3
  60.3 35.8 all-gather.7
  98.1 34.0 all-gather.5
  154.5 46.8 reduce-scatter.18
  204.9 42.5 reduce-scatter.12
  250.8 45.4 reduce-scatter.16
  298.6 19.9 reduce-scatter.20
  320.8 18.1 reduce-scatter.14
  341.2 18.5 reduce-scatter.22

commit v2 on v1

--- a/solution.py
+++ b/solution.py
@@ -1,3 +1,5 @@
+from functools import partial
+
 import jax
 import jax.numpy as jnp
 from jax import lax
@@ -15,6 +17,7 @@
 CONV = DI + 2 * N
 STEP_AT = CONV
 WIDE = CONV + 128
+SPLIT = 896
 STATE = DI + 128
 HALO = 16
 EPSILON = 1e-05
@@ -76,10 +79,35 @@
 
 
 def before_scan(
-    hid, halo, gain, weight, taps, offset, bias, rate,
-    normed_out, normed_halo_out, ext_out, pre_out, conv_out, cum_out, cumt_out,
-    step_out, arg_out, state_out, ext32,
+    plan, me, hid, halo, gain, taps, offset, bias, rate, *refs
 ):
+    pieces = refs[: len(plan)]
+    (
+        normed_out, normed_halo_out, ext_out, pre_out, conv_out, cum_out, cumt_out,
+        step_out, arg_out, state_out, weight_out, ext32, weight, in_sems, out_sem,
+    ) = refs[len(plan) :]
+    keep_weight = pltpu.make_async_copy(weight, weight_out, out_sem)
+
+    @pl.when(pl.program_id(0) == 0)
+    def _():
+        copies = []
+        for piece, (masks, left) in zip(pieces, plan):
+            size, width = piece.shape[0] // len(masks), piece.shape[1]
+            for at, mask in enumerate(masks):
+                row = pl.multiple_of(jnp.bitwise_xor(me[0], mask) * size, size)
+                copies.append(
+                    pltpu.make_async_copy(
+                        piece.at[pl.ds(at * size, size)],
+                        weight.at[pl.ds(row, size), pl.ds(left, width)],
+                        in_sems.at[len(copies)],
+                    )
+                )
+        for copy in copies:
+            copy.start()
+        for copy in copies:
+            copy.wait()
+        keep_weight.start()
+
     def norm(v):
         v = v.astype(F32)
         scale = lax.rsqrt(jnp.mean(v * v, axis=-1, keepdims=True) + EPSILON)
@@ -123,6 +151,10 @@
     keys = conv_out[0, :, DI : DI + N]
     state_out[0, :, :DI] = dot(keys, weighted, (0, 0)).astype(BF)
     state_out[0, :, DI:] = jnp.broadcast_to(last_lanes(last), (N, 128)).astype(BF)
+
+    @pl.when(pl.program_id(0) == pl.num_programs(0) - 1)
+    def _():
+        keep_weight.wait()
 
 
 def within_block(conv, cum, cumt, stept, y_out):
@@ -293,10 +325,130 @@
     d_proj_out[0, :, STEP_AT:] = d_arg.astype(BF)
 
 
-def per_sequence(body, ins, outs, scratch=(), name=None):
+def scan_weight_grad(plan, me, rows, rows_halo, grad, grad_halo, *refs):
+    outs, (total, sems) = refs[: len(plan)], refs[len(plan) :]
+    half = total.shape[1] // 2
+    for left in (0, half):
+        cols = slice(left, left + half)
+        part = dot(rows[...], grad[:, cols], (0, 0))
+        part = part + dot(rows_halo[...], grad_halo[:, cols], (0, 0))
+        total[:, cols] = part.astype(BF)
+    copies = []
+    for out, (masks, left) in zip(outs, plan):
+        size, width = out.shape[0] // len(masks), out.shape[1]
+        for at, mask in enumerate(masks):
+            row = pl.multiple_of(jnp.bitwise_xor(me[0], mask) * size, size)
+            copies.append(
+                pltpu.make_async_copy(
+                    total.at[pl.ds(row, size), pl.ds(left, width)],
+                    out.at[pl.ds(at * size, size)],
+                    sems.at[len(copies)],
+                )
+            )
+    for copy in copies:
+        copy.start()
+    for copy in copies:
+        copy.wait()
+
+
+def trade(v, axis, mask):
+    return lax.ppermute(v, axis, [(i, i ^ mask) for i in range(lax.axis_size(axis))])
+
+
+def mask_order(bits):
+    masks = [0]
+    for bit in reversed(bits):
+        masks = masks + [bit | m for m in masks]
+    return masks
+
+
+def routes():
+    bits = []
+    bit = 2
+    while bit < lax.axis_size("seq"):
+        bits.append(bit)
+        bit *= 2
+    return bits[::-1], bits
+
+
+def paired():
+    seq, head = lax.axis_size("seq"), lax.axis_size("head")
+    return seq & (seq - 1) == 0 and head & (head - 1) == 0 and (D // seq) % 16 == 0
+
+
+def gather_head(v):
+    count, me = lax.axis_size("head"), lax.axis_index("head")
+    parts = [v] + [
+        lax.ppermute(v, "head", [(i, (i - k) % count) for i in range(count)])
+        for k in range(1, count)
+    ]
+    both = jnp.concatenate(parts + parts, axis=0)
+    at = (count - me) * v.shape[0]
+    return lax.dynamic_slice_in_dim(both, at, count * v.shape[0], axis=0)
+
+
+def gather_pieces(v, split):
+    mine = gather_head(v)
+    pieces, plan = [], []
+    for cols, bits, left in (
+        (mine[:, :split], routes()[0], 0),
+        (mine[:, split:], routes()[1], split),
+    ):
+        for bit in bits[::-1]:
+            cols = jnp.concatenate([cols, trade(cols, "seq", bit)], axis=0)
+        masks = mask_order(bits)
+        pieces += [cols, trade(cols, "seq", 1)]
+        plan += [(masks, left), ([m | 1 for m in masks], left)]
+    return pieces, plan
+
+
+def scatter_plan(split):
+    plan = []
+    for extra in (0, 1):
+        for bits, left in zip(routes(), (0, split)):
+            plan.append(([m | extra for m in mask_order(bits)], left))
+    return plan
+
+
+def add(a, b):
+    return (a.astype(F32) + b.astype(F32)).astype(BF)
+
+
+def scatter_pieces(pieces):
+    sums = []
+    for kept, sent, bits in zip(pieces[:2], pieces[2:], routes()):
+        part = add(kept, trade(sent, "seq", 1))
+        for bit in bits:
+            half = part.shape[0] // 2
+            part = add(part[:half], trade(part[half:], "seq", bit))
+        sums.append(part)
+    part = jnp.concatenate(sums, axis=1)
+    count, me = lax.axis_size("head"), lax.axis_index("head")
+    size = part.shape[0] // count
+    total = lax.dynamic_slice_in_dim(part, me * size, size, axis=0).astype(F32)
+    for k in range(1, count):
+        away = lax.dynamic_slice_in_dim(part, lax.rem(me + k, count) * size, size, axis=0)
+        got = lax.ppermute(away, "head", [(i, (i + k) % count) for i in range(count)])
+        total = total + got.astype(F32)
+    return total
+
+
+def sum_all(v):
+    for axis in BOTH:
+        mask = 1
+        while mask < lax.axis_size(axis):
+            v = v + trade(v, axis, mask)
+            mask *= 2
+    return v
+
+
+def per_sequence(body, ins, outs, scratch=(), loose=(), loose_outs=0, name=None):
     seqs = next(v.shape[0] for v in ins if v.ndim == 3)
+    free = pl.BlockSpec(memory_space=pl.ANY)
 
     def spec(shape):
+        if len(shape) == 1:
+            return pl.BlockSpec(memory_space=pltpu.SMEM)
         if len(shape) == 2:
             return pl.BlockSpec(shape, lambda s: (0, 0))
         return pl.BlockSpec((1,) + tuple(shape[1:]), lambda s: (s, 0, 0))
@@ -304,13 +456,14 @@
     return pl.pallas_call(
         body,
         grid=(seqs,),
-        in_specs=[spec(v.shape) for v in ins],
-        out_specs=[spec(shape) for shape, _ in outs],
+        in_specs=[spec(v.shape) for v in ins] + [free] * len(loose),
+        out_specs=[spec(shape) for shape, _ in outs[: len(outs) - loose_outs]]
+        + [free] * loose_outs,
         out_shape=[jax.ShapeDtypeStruct(shape, kind) for shape, kind in outs],
         scratch_shapes=list(scratch),
         compiler_params=PARAMS,
         name=name,
-    )(*ins)
+    )(*ins, *loose)
 
 
 def scan_states(parts, groups, blocks, reverse):
@@ -405,9 +558,18 @@
     backward = [(i + near, i) for i in range(devices - near)]
 
     halo = lax.ppermute(hidden[:, CH - HALO :], BOTH, onward)
-    w_gate = gather_rows(input_projection_weight[:, :DI])
-    w_scan = gather_rows(pad_lanes(input_projection_weight[:, DI:], WIDE))
-    w_out = gather_rows(output_projection_weight)
+    fast = paired()
+    me = lax.axis_index("seq").astype(jnp.int32)[None]
+    scan_part = pad_lanes(input_projection_weight[:, DI:], WIDE)
+    other_part = jnp.concatenate([input_projection_weight[:, :DI], output_projection_weight], 1)
+    if fast:
+        pieces, plan = gather_pieces(scan_part, SPLIT)
+        others = lax.all_gather(gather_head(other_part), "seq", axis=0, tiled=True)
+    else:
+        pieces, plan = [gather_rows(scan_part)], [([0], 0)]
+        me = jnp.zeros_like(me)
+        others = gather_rows(other_part)
+    w_gate, w_out = others[:, :DI], others[:, DI:]
 
     gain_one = norm_gain[None]
     gain_two = gate_gain[None]
@@ -417,9 +579,9 @@
     rate = pad_lanes(-jnp.exp(decay_log)[None], 128)
     skip = jnp.repeat(skip_weight, P_SIZE)[None]
 
-    (normed, normed_halo, ext, pre, conv, cum, cumt, step, arg, parts) = per_sequence(
-        before_scan,
-        [hidden, halo, gain_one, w_scan, taps, offset, bias, rate],
+    (normed, normed_halo, ext, pre, conv, cum, cumt, step, arg, parts, w_scan) = per_sequence(
+        partial(before_scan, plan),
+        [me, hidden, halo, gain_one, taps, offset, bias, rate],
         [
             ((seqs, CH, D), BF),
             ((seqs, HALO, D), BF),
@@ -431,8 +593,16 @@
             ((seqs, CH, 128), F32),
             ((seqs, CH, 128), F32),
             ((seqs, N, STATE), BF),
+            ((D, WIDE), BF),
         ],
-        [pltpu.VMEM((HALO + CH, CONV), F32)],
+        [
+            pltpu.VMEM((HALO + CH, CONV), F32),
+            pltpu.VMEM((D, WIDE), BF),
+            pltpu.SemaphoreType.DMA((sum(len(masks) for masks, _ in plan),)),
+            pltpu.SemaphoreType.DMA,
+        ],
+        loose=pieces,
+        loose_outs=1,
         name="before_scan",
     )
     starts = scan_states(parts, scan_groups, blocks, False)
@@ -466,8 +636,14 @@
     widened = hidden.astype(F32)
     mixed = (widened + branch).astype(BF)
     d_gate_rows = d_gate.reshape(tokens, DI)
-    out_rows = scatter_rows(dot(cotangent, mixed_rows, (0, 0)).astype(BF))
-    gate_rows = scatter_rows(dot(normed_rows, d_gate_rows, (0, 0)).astype(BF))
+    other_term = jnp.concatenate(
+        [
+            dot(normed_rows, d_gate_rows, (0, 0)).astype(BF),
+            dot(cotangent, mixed_rows, (0, 0)).astype(BF),
+        ],
+        axis=1,
+    )
+    other_rows = scatter_rows(other_term)
 
     dx_within, d_keys, d_queries = per_sequence(
         within_block_back,
@@ -493,10 +669,31 @@
     )
     d_scan_rows = d_scan.reshape(tokens, WIDE)
     d_halo_rows = d_halo.reshape(seqs * HALO, WIDE)
-    scan_term = dot(normed_rows, d_scan_rows, (0, 0)) + dot(
-        normed_halo.reshape(seqs * HALO, D), d_halo_rows, (0, 0)
-    )
-    scan_rows = scatter_rows(scan_term.astype(BF))
+    normed_halo_rows = normed_halo.reshape(seqs * HALO, D)
+    plan = scatter_plan(SPLIT) if fast else [([0], 0)]
+    terms = pl.pallas_call(
+        partial(scan_weight_grad, plan),
+        in_specs=[pl.BlockSpec(memory_space=pltpu.SMEM)]
+        + [pl.BlockSpec(memory_space=pltpu.VMEM)] * 4,
+        out_specs=[pl.BlockSpec(memory_space=pl.ANY)] * len(plan),
+        out_shape=[
+            jax.ShapeDtypeStruct(
+                (
+                    D // lax.axis_size("seq") * len(masks) if fast else D,
+                    (WIDE - SPLIT if left else SPLIT) if fast else WIDE,
+                ),
+                BF,
+            )
+            for masks, left in plan
+        ],
+        scratch_shapes=[
+            pltpu.VMEM((D, WIDE), BF),
+            pltpu.SemaphoreType.DMA((sum(len(masks) for masks, _ in plan),)),
+        ],
+        compiler_params=PARAMS,
+        name="scan_weight_grad",
+    )(me, normed_rows, normed_halo_rows, d_scan_rows, d_halo_rows)
+    scan_rows = scatter_pieces(terms) if fast else scatter_rows(terms[0])
 
     d_normed_halo = dot(d_halo_rows, w_scan, (1, 1)).reshape(seqs, HALO, D)
     from_next = lax.ppermute(d_normed_halo[:, HALO - 8 :], BOTH, backward)
@@ -526,12 +723,13 @@
         jnp.sum(row_sums[1].reshape(H, P_SIZE), axis=1),
         row_sums[0],
     )
-    summed = lax.psum(jnp.concatenate(pieces), BOTH)
+    flat = jnp.concatenate(pieces)
+    summed = sum_all(jnp.pad(flat, (0, -flat.shape[0] % 1024))) if fast else lax.psum(flat, BOTH)
     outs, at = [], 0
     for piece in pieces:
         outs.append(summed[at : at + piece.shape[0]])
         at += piece.shape[0]
-    in_rows = jnp.concatenate([gate_rows, scan_rows[:, : CONV + H]], axis=1)
+    in_rows = jnp.concatenate([other_rows[:, :DI], scan_rows[:, : CONV + H]], axis=1)
     return (
         mixed,
         hidden_grad,
@@ -543,7 +741,7 @@
         outs[4],
         outs[5],
         outs[6],
-        out_rows,
+        other_rows[:, DI:],
     )
 
 

time: 369 us -> 314 us (0.85)
  blocking collectives: 117 us -> 27 us
  starting transfers between devices: 17.6 us -> 55.4 us
  waiting for transfers between devices: 98.6 us -> 85.9 us
  other arithmetic: 4.2 us -> 15 us
  matrix products: 38 us -> 28.9 us
  Pallas kernels: 59.8 us -> 67.7 us
    ppermute x0 -> x26, waiting for transfers between devices: none -> 53.4 us  [the longest x17 31.8 us: trade(): lax.ppermute(v, axis, [(i, i ^ mask) for i in range(lax.axis_size(axis))])]
    all_gather x3 -> x0, blocking collectives: 48.5 us -> none  [gather_rows(): lax.all_gather(v, 'head', axis=0, tiled=True)]
    psum x1 -> x0, blocking collectives: 41.5 us -> none  [on_device(): summed = lax.psum(jnp.concatenate(pieces), BOTH)]
    unnamed x12 -> x3, waiting for transfers between devices: 41.1 us -> 0.05 us
    ppermute x0 -> x26, starting transfers between devices: none -> 34.3 us  [the longest x17 17.8 us: trade(): lax.ppermute(v, axis, [(i, i ^ mask) for i in range(lax.axis_size(axis))])]
    reduce_scatter x1, waiting for transfers between devices: 18.5 us -> 4.63 us  [scatter_rows(): part = lax.psum_scatter(part, 'head', scatter_dimension=0, tiled=True)]
    all_gather x3 -> x1, waiting for transfers between devices: 10.5 us -> 0.01 us  [on_device(): others = lax.all_gather(gather_head(other_part), 'seq', axis=0, tiled=True)]
    pallas_call x5 -> x6, Pallas kernels: 54.7 us -> 62.6 us  [the longest x5 56.4 us: per_sequence(): pl.pallas_call(body, grid=(seqs,), in_specs=[spec(v.shape) for v in ins]...]
  transfers between devices with their start and end apart: 14 -> 34, of which waited for: 8 -> 19; matrix products, arithmetic and copies ran while one was open for 13% -> 15% of each run, Pallas kernels for 13% -> 18%
where the time goes in v2:
time: 314 us; the launch traced here: 312 us
  waiting for transfers between devices  85.9 us (27%)
  Pallas kernels  67.7 us (22%)
  starting transfers between devices  55.4 us (18%)
  matrix products  28.9 us (9%)
  blocking collectives  27 us (9%)
  local copies, waits for them, and re-layouts  18.1 us (6%)
  other arithmetic  15 us (5%)
  between operations  14.5 us (5%)
    pallas_call x5, Pallas kernels, per_sequence(): pl.pallas_call(body, grid=(seqs,), in_specs=[spec(v.shape) for v in ins]...  56.4 us
    ppermute x17, waiting for transfers between devices, trade(): lax.ppermute(v, axis, [(i, i ^ mask) for i in range(lax.axis_size(axis))])  31.8 us
    all_to_all x1, blocking collectives, scan_states(): lax.all_to_all(parts.reshape(seqs * N, STATE), BOTH, split_axis=0, concat...  27 us
    dot_general x6, matrix products, dot(): lax.dot_general(a, b, (((contract[0],), (contract[1],)), ((), ())), prefe...  21 us
    ppermute x17, starting transfers between devices, trade(): lax.ppermute(v, axis, [(i, i ^ mask) for i in range(lax.axis_size(axis))])  17.8 us
    ppermute x6, waiting for transfers between devices, gather_head(): lax.ppermute(v, 'head', [(i, (i - k) % count) for i in range(count)])  17.4 us
    all_to_all x1, waiting for transfers between devices, scan_states(): lax.all_to_all(parts.reshape(seqs * N, STATE), BOTH, split_axis=0, concat...  15.1 us
    all_to_all x2, waiting for transfers between devices, scan_states(): lax.all_to_all(out.reshape(seqs * N, DI), BOTH, split_axis=0, concat_axis...  12.7 us
  transfers between devices with their start and end apart: 34, of which 19 were waited for; matrix products, arithmetic and copies ran while one was open for 15% of the time, Pallas kernels for 18%

profile of v2, /device:TPU:0, one launch (start us, length us, event | category | flops | bytes accessed | tf_op | source)
XLA Modules:
  0.0 312.4 jit_solution(15007124585247732562)
XLA Ops:
  9.0 5.1 %collective-permute-start.10 = (bf16[24,3072]{1,0:T(8,128)(2,1)S(1)}, bf16[24,3072]{1,0:T(8,128)(2,1)S(1)}, u32[]{:S(2)}, u32[]{:S(2)}) collective-permute-start(bf16[24,3072]{1,0:T(8,128)(2,1)S(1)} %get-tuple-element.76), channel_id=1, source_target_pairs={{0,3},{1,0},{2,1},{3,2},{4,7},{5,4},{6,5},{7,6},{8,11},{9,8},{10,9... | collective-permute-start | bytes 442376 | tf_op jit(solution)/shard_map/ppermute | solution.py:382
  14.1 1.0 collective-permute-start.12
  15.1 3.3 %collective-permute-done.10 = bf16[24,3072]{1,0:T(8,128)(2,1)S(1)} collective-permute-done((bf16[24,3072]{1,0:T(8,128)(2,1)S(1)}, bf16[24,3072]{1,0:T(8,128)(2,1)S(1)}, u32[]{:S(2)}, u32[]{:S(2)}) %collective-permute-start.10) | collective-permute-done | bytes 147488 | tf_op jit(solution)/shard_map/ppermute | solution.py:382
  18.4 8.2 %collective-permute-done.11 = bf16[24,3072]{1,0:T(8,128)(2,1)S(1)} collective-permute-done((bf16[24,3072]{1,0:T(8,128)(2,1)S(1)}, bf16[24,3072]{1,0:T(8,128)(2,1)S(1)}, u32[]{:S(2)}, u32[]{:S(2)}) %collective-permute-start.11) | collective-permute-done | bytes 147488 | tf_op jit(solution)/shard_map/ppermute | solution.py:382
  26.7 0.9 constant_dynamic-update-slice_fusion.11
  27.7 0.9 constant_dynamic-slice_fusion.1
  28.7 1.5 collective-permute-start.1
  30.1 1.4 collective-permute-start.2
  31.5 1.9 collective-permute-start.3
  34.2 5.2 %collective-permute-done.2 = bf16[24,1920]{1,0:T(8,128)(2,1)S(1)} collective-permute-done((bf16[24,1920]{1,0:T(8,128)(2,1)S(1)}, bf16[24,1920]{1,0:T(8,128)(2,1)S(1)}, u32[]{:S(2)}, u32[]{:S(2)}) %collective-permute-start.2) | collective-permute-done | bytes 92192 | tf_op jit(solution)/shard_map/ppermute | solution.py:382
  39.6 1.6 collective-permute-start.7
  41.2 1.6 collective-permute-start.4
  42.7 7.2 %collective-permute-done.7 = bf16[96,1024]{1,0:T(8,128)(2,1)S(1)} collective-permute-done((bf16[96,1024]{1,0:T(8,128)(2,1)S(1)}, bf16[96,1024]{1,0:T(8,128)(2,1)S(1)}, u32[]{:S(2)}, u32[]{:S(2)}) %collective-permute-start.7) | collective-permute-done | bytes 196640 | tf_op jit(solution)/shard_map/ppermute | solution.py:355
  50.0 1.7 collective-permute-start.8
  52.5 7.0 %collective-permute-done.8 = bf16[192,1024]{1,0:T(8,128)(2,1)S(1)} collective-permute-done((bf16[192,1024]{1,0:T(8,128)(2,1)S(1)}, bf16[192,1024]{1,0:T(8,128)(2,1)S(1)}, u32[]{:S(2)}, u32[]{:S(2)}) %collective-permute-start.8) | collective-permute-done | bytes 393248 | tf_op jit(solution)/shard_map/ppermute | solution.py:355
  59.6 1.9 collective-permute-done.5
  62.5 5.8 %collective-permute-start = (bf16[2,16,768]{2,1,0:T(8,128)(2,1)S(1)}, bf16[2,16,768]{2,1,0:T(8,128)(2,1)S(1)}, u32[]{:S(2)}, u32[]{:S(2)}) collective-permute-start(bf16[2,16,768]{2,1,0:T(8,128)(2,1)S(1)} %slice.99), channel_id=1, source_target_pairs={{0,1},{1,2},{2,3},{3,4},{4,5},{5,6},{6,7},{7,8},{8,9},{9,10},{10,1... | collective-permute-start | bytes 147464 | tf_op jit(solution)/shard_map/ppermute | solution.py:560
  72.4 12.8 %before_scan.1 = (bf16[2,256,768]{2,1,0:T(8,128)(2,1)}, bf16[2,16,768]{2,1,0:T(8,128)(2,1)}, bf16[2,272,1792]{2,1,0:T(8,128)(2,1)}, f32[2,256,1792]{2,1,0:T(8,12...) custom-call(s32[1]{0:T(128)} %bitcast.me, ...), custom_call_target="tpu_custom_call" | custom-call | tf_op jit(solution)/shard_map/before_scan/pallas_call | solution.py:456
  85.2 27.0 %all_to_all.30.refs_0_ = bf16[32,8,1664]{2,1,0:T(8,128)(2,1)} all-to-all(bf16[32,8,1664]{2,1,0:T(8,128)(2,1)} %bitcast.62), channel_id=1, replica_groups=mesh['seq'=8,'head'=4] {'seq','head'}, dimensions={0} | all-to-all | bytes 1703936 | tf_op jit(solution)/shard_map/all_to_all | solution.py:472
  112.2 2.5 state_scan.2
  114.8 4.6 %all-to-all-start.1 = ((bf16[32,8,1536]{2,1,0:T(8,128)(2,1)}), bf16[32,8,1536]{2,1,0:T(8,128)(2,1)S(1)}, u32[]{:S(2)}, u32[]{:S(2)}) async-start(bf16[32,8,1536]{2,1,0:T(8,128)(2,1)} %state_scan.2), calls=%async_computation.1 | async-start | bytes 1572864 | tf_op jit(solution)/shard_map/all_to_all | solution.py:498
  121.5 5.4 %within_block.1.within = f32[2,256,1536]{2,1,0:T(8,128)} custom-call(bf16[2,256,1792]{2,1,0:T(8,128)(2,1)} %get-tuple-element.39.conv, f32[2,256,128]{2,1,0:T(8,128)} %get-tuple-element.40.cum, f32[2,32,256]{2,1,0:T(8,128)} %get-tuple-element.41.cumt, f32[2,32,256]{2,1,0:T(8,128)} %slice.133.stept), custom_call_target="tpu_custom_call" | custom-call | tf_op jit(solution)/shard_map/within_block/pallas_call | solution.py:456
  126.9 4.8 %fusion.5.gate = f32[2,256,1536]{2,1,0:T(8,128)} fusion(bf16[2,256,768]{2,1,0:T(8,128)(2,1)S(1)} %copy-done.11, bf16[768,3072]{1,0:T(8,128)(2,1)} %all-gather.2.cloned.1.call-done), kind=kOutput, calls=%fused_computation.11 | convolution fusion | flops 1207959552 | bytes 6291456 | tf_op jit(solution)/shard_map/dot_general | solution.py:615
  131.7 3.1 fusion.11
  134.8 4.0 %all-to-all-done.1 = bf16[32,8,1536]{2,1,0:T(8,128)(2,1)S(1)} async-done(((bf16[32,8,1536]{2,1,0:T(8,128)(2,1)}), bf16[32,8,1536]{2,1,0:T(8,128)(2,1)S(1)}, u32[]{:S(2)}, u32[]{:S(2)}) %all-to-all-start.1) | async-done | bytes 786464 | tf_op jit(solution)/shard_map/all_to_all | solution.py:498
  139.6 11.1 %around_norm.1 = (bf16[2,256,1536]{2,1,0:T(8,128)(2,1)}, bf16[2,256,1536]{2,1,0:T(8,128)(2,1)}, bf16[2,256,1536]{2,1,0:T(8,128)(2,1)}, f32[2,256,128]{2,1,0:T(8,...) custom-call(f32[2,256,1536]{2,1,0:T(8,128)} %within_block.1.within, ...), custom_call_target="tpu_custom_call" | custom-call | tf_op jit(solution)/shard_map/around_norm/pallas_call | solution.py:456
  150.8 4.2 %bitcast_convert_fusion.1 = bf16[768,1536]{1,0:T(8,128)(2,1)} fusion(bf16[2,256,768]{2,1,0:T(8,128)(2,1)S(1)} %copy-done.11, bf16[2,256,1536]{2,1,0:T(8,128)(2,1)} %get-tuple-element.46), kind=kOutput, calls=%fused_computation.2 | convolution fusion | flops 1209139200 | bytes 4718592 | tf_op jit(solution)/shard_map/dot_general | solution.py:31
  155.0 4.4 %all-to-all-start.2 = ((bf16[32,8,1664]{2,1,0:T(8,128)(2,1)}), bf16[32,8,1664]{2,1,0:T(8,128)(2,1)S(1)}, u32[]{:S(2)}, u32[]{:S(2)}) async-start(bf16[32,8,1664]{2,1,0:T(8,128)(2,1)} %bitcast.12), calls=%async_computation.2 | async-start | bytes 1703936 | tf_op jit(solution)/shard_map/all_to_all | solution.py:472
  159.4 3.0 fusion
  162.4 2.8 pad_maximum_fusion
  165.2 15.1 %all-to-all-done.2.refs_0_ = bf16[32,8,1664]{2,1,0:T(8,128)(2,1)S(1)} async-done(((bf16[32,8,1664]{2,1,0:T(8,128)(2,1)}), bf16[32,8,1664]{2,1,0:T(8,128)(2,1)S(1)}, u32[]{:S(2)}, u32[]{:S(2)}) %all-to-all-start.2) | async-done | bytes 852000 | tf_op jit(solution)/shard_map/all_to_all | solution.py:472
  181.3 2.6 state_scan.3
  183.8 4.4 %all-to-all-start.3 = ((bf16[32,8,1536]{2,1,0:T(8,128)(2,1)}), bf16[32,8,1536]{2,1,0:T(8,128)(2,1)S(1)}, u32[]{:S(2)}, u32[]{:S(2)}) async-start(bf16[32,8,1536]{2,1,0:T(8,128)(2,1)} %state_scan.3), calls=%async_computation.3 | async-start | bytes 1572864 | tf_op jit(solution)/shard_map/all_to_all | solution.py:498
  188.8 9.6 %within_block_back.1 = (f32[2,256,1536]{2,1,0:T(8,128)}, f32[2,256,128]{2,1,0:T(8,128)}, f32[2,256,128]{2,1,0:T(8,128)}) custom-call(bf16[2,256,1792]{2,1,0:T(8,128)(2,1)} %get-tuple-element.39.conv, f32[2,256,128]{2,1,0:T(8,128)} %get-tuple-element.40.cum, f32[2,32,256]{2,1,0:T(8,128)} %get-tuple-element.41.cumt, f32[2,256,128]{2,1,0:T(8,128)} %get-tuple-element.42.step, ...), custom_call_target="tpu_custom_call" | custom-call | tf_op jit(solution)/shard_map/within_block_back/pallas_call | solution.py:456
  199.1 8.7 %all-to-all-done.3 = bf16[32,8,1536]{2,1,0:T(8,128)(2,1)S(1)} async-done(((bf16[32,8,1536]{2,1,0:T(8,128)(2,1)}), bf16[32,8,1536]{2,1,0:T(8,128)(2,1)S(1)}, u32[]{:S(2)}, u32[]{:S(2)}) %all-to-all-start.3) | async-done | bytes 786464 | tf_op jit(solution)/shard_map/all_to_all | solution.py:498
  208.7 17.4 %after_scan.1 = (bf16[2,256,1920]{2,1,0:T(8,128)(2,1)}, bf16[2,16,1920]{2,1,0:T(8,128)(2,1)}, f32[2,8,1792]{2,1,0:T(8,128)}, f32[2,8,128]{2,1,0:T(8,128)}) custom-call(bf16[2,256,1792]{2,1,0:T(8,128)(2,1)} %get-tuple-element.39.conv, f32[2,256,1792]{2,1,0:T(8,128)} %get-tuple-element.47.pre, bf16[2,272,1792]{2,1,0:T(8,128)(2,1)} %get-tuple-element.48.ext, ...), custom_call_target="tpu_custom_call" | custom-call | tf_op jit(solution)/shard_map/after_scan/pallas_call | solution.py:456
  226.1 2.5 fusion.1
  228.6 1.5 collective-permute-start.13
  230.1 1.5 reduce_sum.66
  231.7 1.3 reduce_sum.67
  233.0 1.3 slice_bitcast_fusion
  234.3 3.8 %fusion.36 = f32[512,768]{1,0:T(8,128)S(1)} fusion(bf16[512,1920]{1,0:T(8,128)(2,1)S(1)} %bitcast.61, bf16[768,1920]{1,0:T(8,128)(2,1)} %get-tuple-element.57), kind=kOutput, calls=%fused_computation.87 | convolution fusion | flops 1509949440 | bytes 6488064 | tf_op jit(solution)/shard_map/dot_general | solution.py:31
  238.1 3.1 %fusion.25 = f32[512,768]{1,0:T(8,128)S(1)} fusion(f32[512,768]{1,0:T(8,128)S(1)} %fusion.36, bf16[512,1536]{1,0:T(8,128)(2,1)S(1)} %bitcast.68, bf16[768,3072]{1,0:T(8,128)(2,1)} %all-gather.2.cloned.1.call-done), kind=kOutput, calls=%fused_computation.31 | convolution fusion | flops 1208352768 | bytes 7077888 | tf_op jit(solution)/shard_map/dot_general | solution.py:31
  241.3 1.3 fusion.20
  242.8 4.0 %collective-permute-start.14 = (f32[12288]{0:T(1024)S(1)}, f32[12288]{0:T(1024)S(1)}, u32[]{:S(2)}, u32[]{:S(2)}) collective-permute-start(f32[12288]{0:T(1024)S(1)} %pad.28), channel_id=1, source_target_pairs={{0,4},{4,0},{8,12},{12,8},{16,20},{20,16},{24,28},{28,24},{1,5},{5... | collective-permute-start | bytes 147464 | tf_op jit(solution)/shard_map/ppermute | solution.py:355
  247.7 1.5 collective-permute-start.15
  249.1 6.3 %scan_weight_grad.1 = (bf16[384,896]{1,0:T(8,128)(2,1)}, bf16[384,1024]{1,0:T(8,128)(2,1)}, bf16[384,896]{1,0:T(8,128)(2,1)}, bf16[384,1024]{1,0:T(8,128)(2,1)}) custom-call(s32[1]{0:T(128)} %bitcast.me, bf16[512,768]{1,0:T(8,128)(2,1)} %bitcast.64, bf16[32,768]{1,0:T(8,128)(2,1)} %bitcast.67, bf16[512,1920]{1,0:T(8,128)(2,1)} %bitcast.60, ...), custom_call_target="tpu_custom_call" | custom-call | tf_op jit(solution)/shard_map/scan_weight_grad/pallas_call | solution.py:674
  256.7 4.4 %fusion.21 = bf16[2,256,768]{2,1,0:T(8,128)(2,1)} fusion(bf16[2,256,768]{2,1,0:T(8,128)(2,1)S(1)} %copy-done, bf16[2,256,1536]{2,1,0:T(8,128)(2,1)} %get-tuple-element.45, bf16[768,3072]{1,0:T(8,128)(2,1)} %all-gather.2.cloned.1.call-done), kind=kOutput, calls=%fused_computation.27 | convolution fusion | flops 1209139200 | bytes 5505024 | tf_op jit(solution)/shard_map/dot_general | solution.py:31
  261.3 4.1 %collective-permute-done.17 = f32[12288]{0:T(1024)S(1)} collective-permute-done((f32[12288]{0:T(1024)S(1)}, f32[12288]{0:T(1024)S(1)}, u32[]{:S(2)}, u32[]{:S(2)}) %collective-permute-start.17) | collective-permute-done | bytes 49184 | tf_op jit(solution)/shard_map/ppermute | solution.py:355
  265.9 1.3 add_convert_fusion.1
  267.3 1.0 collective-permute-start.20
  268.6 2.0 collective-permute-start.23
  270.5 2.4 fusion.19
  273.0 2.7 collective-permute-done.20
  275.8 1.5 collective-permute-start.21
  277.3 2.7 collective-permute-done.23
  280.5 1.3 collective-permute-done.21
  281.8 4.0 %collective-permute-done.24 = bf16[96,1024]{1,0:T(8,128)(2,1)S(1)} collective-permute-done((bf16[96,1024]{1,0:T(8,128)(2,1)S(1)}, bf16[96,1024]{1,0:T(8,128)(2,1)S(1)}, u32[]{:S(2)}, u32[]{:S(2)}) %collective-permute-start.24) | collective-permute-done | bytes 196640 | tf_op jit(solution)/shard_map/ppermute | solution.py:355
  285.9 1.0 collective-permute-start.25
  286.9 2.0 collective-permute-start.26
  288.9 2.6 collective-permute-start.27
  294.6 3.6 %collective-permute-done.26 = bf16[24,1920]{1,0:T(8,128)(2,1)S(1)} collective-permute-done((bf16[24,1920]{1,0:T(8,128)(2,1)S(1)}, bf16[24,1920]{1,0:T(8,128)(2,1)S(1)}, u32[]{:S(2)}, u32[]{:S(2)}) %collective-permute-start.26) | collective-permute-done | bytes 92192 | tf_op jit(solution)/shard_map/ppermute | solution.py:431
  298.9 4.6 %reduce-scatter.5.cloned.1.call-done = bf16[24,3072]{1,0:T(8,128)(2,1)} async-done(((bf16[96,3072]{1,0:T(8,128)(2,1)}), bf16[24,3072]{1,0:T(8,128)(2,1)}) %reduce-scatter.5.cloned.1.call-update) | async-done | bytes 147472 | tf_op jit(solution)/shard_map/reduce_scatter | solution.py:515
  303.5 1.6 fusion.33
  (169 shorter events, 23.4 us)
Async XLA Ops:
  7.2 119.7 %all-gather.2.cloned.1.call-start = ((), (), s32[]{:S(2)}) async-start(), calls=%async_computation.6 | async-start | bytes 5308416 | tf_op jit(solution)/shard_map/all_gather | solution.py:567
  9.0 9.4 %collective-permute-start.10 = (bf16[24,3072]{1,0:T(8,128)(2,1)S(1)}, bf16[24,3072]{1,0:T(8,128)(2,1)S(1)}, u32[]{:S(2)}, u32[]{:S(2)}) collective-permute-start(bf16[24,3072]{1,0:T(8,128)(2,1)S(1)} %get-tuple-element.76), channel_id=1, source_target_pairs={{0,3},{1,0},{2,1},{3,2},{4,7},{5,4},{6,5},{7,6},{8,11},{9,8},{10,9... | collective-permute-start | bytes 442376 | tf_op jit(solution)/shard_map/ppermute | solution.py:382
  14.1 12.5 %collective-permute-start.11 = (bf16[24,3072]{1,0:T(8,128)(2,1)S(1)}, bf16[24,3072]{1,0:T(8,128)(2,1)S(1)}, u32[]{:S(2)}, u32[]{:S(2)}) collective-permute-start(bf16[24,3072]{1,0:T(8,128)(2,1)S(1)} %get-tuple-element.76), channel_id=1, source_target_pairs={{0,2},{1,3},{2,0},{3,1},{4,6},{5,7},{6,4},{7,5},{8,10},{9,11},{10,... | collective-permute-start | bytes 442376 | tf_op jit(solution)/shard_map/ppermute | solution.py:382
  14.1 12.5 %collective-permute-start.12 = (bf16[24,3072]{1,0:T(8,128)(2,1)S(1)}, bf16[24,3072]{1,0:T(8,128)(2,1)S(1)}, u32[]{:S(2)}, u32[]{:S(2)}) collective-permute-start(bf16[24,3072]{1,0:T(8,128)(2,1)S(1)} %get-tuple-element.76), channel_id=1, source_target_pairs={{0,1},{1,2},{2,3},{3,0},{4,5},{5,6},{6,7},{7,4},{8,9},{9,10},{10,1... | collective-permute-start | bytes 442376 | tf_op jit(solution)/shard_map/ppermute | solution.py:382
  26.6 2.0 copy-start.16
  28.7 5.5 %collective-permute-start.1 = (bf16[24,1920]{1,0:T(8,128)(2,1)S(1)}, bf16[24,1920]{1,0:T(8,128)(2,1)S(1)}, u32[]{:S(2)}, u32[]{:S(2)}) collective-permute-start(bf16[24,1920]{1,0:T(8,128)(2,1)S(1)} %get-tuple-element.78), channel_id=1, source_target_pairs={{0,3},{1,0},{2,1},{3,2},{4,7},{5,4},{6,5},{7,6},{8,11},{9,8},{10,9... | collective-permute-start | bytes 276488 | tf_op jit(solution)/shard_map/ppermute | solution.py:382
  30.1 9.3 %collective-permute-start.2 = (bf16[24,1920]{1,0:T(8,128)(2,1)S(1)}, bf16[24,1920]{1,0:T(8,128)(2,1)S(1)}, u32[]{:S(2)}, u32[]{:S(2)}) collective-permute-start(bf16[24,1920]{1,0:T(8,128)(2,1)S(1)} %get-tuple-element.78), channel_id=1, source_target_pairs={{0,2},{1,3},{2,0},{3,1},{4,6},{5,7},{6,4},{7,5},{8,10},{9,11},{10,... | collective-permute-start | bytes 276488 | tf_op jit(solution)/shard_map/ppermute | solution.py:382
  31.5 7.9 %collective-permute-start.3 = (bf16[24,1920]{1,0:T(8,128)(2,1)S(1)}, bf16[24,1920]{1,0:T(8,128)(2,1)S(1)}, u32[]{:S(2)}, u32[]{:S(2)}) collective-permute-start(bf16[24,1920]{1,0:T(8,128)(2,1)S(1)} %get-tuple-element.78), channel_id=1, source_target_pairs={{0,1},{1,2},{2,3},{3,0},{4,5},{5,6},{6,7},{7,4},{8,9},{9,10},{10,1... | collective-permute-start | bytes 276488 | tf_op jit(solution)/shard_map/ppermute | solution.py:382
  39.6 10.4 %collective-permute-start.7 = (bf16[96,1024]{1,0:T(8,128)(2,1)S(1)}, bf16[96,1024]{1,0:T(8,128)(2,1)S(1)}, u32[]{:S(2)}, u32[]{:S(2)}) collective-permute-start(bf16[96,1024]{1,0:T(8,128)(2,1)S(1)} %dynamic-slice.1), channel_id=1, source_target_pairs={{0,16},{4,20},{8,24},{12,28},{16,0},{20,4},{24,8},{28,12},{1,17},{... | collective-permute-start | bytes 589832 | tf_op jit(solution)/shard_map/ppermute | solution.py:355
  41.2 10.5 %collective-permute-start.4 = (bf16[96,896]{1,0:T(8,128)(2,1)S(1)}, bf16[96,896]{1,0:T(8,128)(2,1)S(1)}, u32[]{:S(2)}, u32[]{:S(2)}) collective-permute-start(bf16[96,896]{1,0:T(8,128)(2,1)S(1)} %constant_dynamic-slice_fusion), channel_id=1, source_target_pairs={{0,8},{4,12},{8,0},{12,4},{16,24},{20,28},{24,16},{28,20},{1,9},{5... | collective-permute-start | bytes 516104 | tf_op jit(solution)/shard_map/ppermute | solution.py:355
  50.0 9.5 %collective-permute-start.8 = (bf16[192,1024]{1,0:T(8,128)(2,1)S(1)}, bf16[192,1024]{1,0:T(8,128)(2,1)S(1)}, u32[]{:S(2)}, u32[]{:S(2)}) collective-permute-start(bf16[192,1024]{1,0:T(8,128)(2,1)S(1)} %pad_maximum_fusion.3), channel_id=1, source_target_pairs={{0,8},{4,12},{8,0},{12,4},{16,24},{20,28},{24,16},{28,20},{1,9},{5... | collective-permute-start | bytes 1179656 | tf_op jit(solution)/shard_map/ppermute | solution.py:355
  51.8 16.6 %copy-start.30 = (f32[24]{0:T(128)S(1)}, f32[24]{0:T(128)}, u32[]{:S(2)}) copy-start(f32[24]{0:T(128)} %param.18) | copy-start | bytes 292
  51.8 16.6 %copy-start.21 = (f32[4,1792]{1,0:T(4,128)S(1)}, f32[4,1792]{1,0:T(4,128)}, u32[]{:S(2)}) copy-start(f32[4,1792]{1,0:T(4,128)} %param.15) | copy-start | bytes 86020
  51.8 17.8 %copy-start.23 = (f32[1792]{0:T(1024)S(1)}, f32[1792]{0:T(1024)}, u32[]{:S(2)}) copy-start(f32[1792]{0:T(1024)} %param.16) | copy-start | bytes 21508
  51.8 18.3 %copy-start.20 = (f32[768]{0:T(1024)S(1)}, f32[768]{0:T(1024)}, u32[]{:S(2)}) copy-start(f32[768]{0:T(1024)} %param.13) | copy-start | bytes 9220
  51.8 18.9 %copy-start.31 = (f32[24]{0:T(128)S(1)}, f32[24]{0:T(128)}, u32[]{:S(2)}) copy-start(f32[24]{0:T(128)} %param.17) | copy-start | bytes 292
  51.8 9.7 %collective-permute-start.5 = (bf16[192,896]{1,0:T(8,128)(2,1)S(1)}, bf16[192,896]{1,0:T(8,128)(2,1)S(1)}, u32[]{:S(2)}, u32[]{:S(2)}) collective-permute-start(bf16[192,896]{1,0:T(8,128)(2,1)S(1)} %pad_maximum_fusion.4), channel_id=1, source_target_pairs={{0,16},{4,20},{8,24},{12,28},{16,0},{20,4},{24,8},{28,12},{1,17},{... | collective-permute-start | bytes 1032200 | tf_op jit(solution)/shard_map/ppermute | solution.py:355
  59.5 11.8 %copy-start.4 = (bf16[384,1024]{1,0:T(8,128)(2,1)}, bf16[384,1024]{1,0:T(8,128)(2,1)S(1)}, u32[]{:S(2)}) copy-start(bf16[384,1024]{1,0:T(8,128)(2,1)S(1)} %pad_maximum_fusion.1.refs_2_) | copy-start | bytes 2359300
  59.5 11.7 %collective-permute-start.9 = (bf16[384,1024]{1,0:T(8,128)(2,1)S(1)}, bf16[384,1024]{1,0:T(8,128)(2,1)S(1)}, u32[]{:S(2)}, u32[]{:S(2)}) collective-permute-start(bf16[384,1024]{1,0:T(8,128)(2,1)S(1)} %pad_maximum_fusion.1.refs_2_), channel_id=1, source_target_pairs={{0,4},{4,0},{8,12},{12,8},{16,20},{20,16},{24,28},{28,24},{1,5},{5... | collective-permute-start | bytes 2359304 | tf_op jit(solution)/shard_map/ppermute | solution.py:355
  61.6 9.7 %copy-start.6 = (bf16[384,896]{1,0:T(8,128)(2,1)}, bf16[384,896]{1,0:T(8,128)(2,1)S(1)}, u32[]{:S(2)}) copy-start(bf16[384,896]{1,0:T(8,128)(2,1)S(1)} %pad_maximum_fusion.2.refs_0_) | copy-start | bytes 2064388
  61.6 9.7 %collective-permute-start.6 = (bf16[384,896]{1,0:T(8,128)(2,1)S(1)}, bf16[384,896]{1,0:T(8,128)(2,1)S(1)}, u32[]{:S(2)}, u32[]{:S(2)}) collective-permute-start(bf16[384,896]{1,0:T(8,128)(2,1)S(1)} %pad_maximum_fusion.2.refs_0_), channel_id=1, source_target_pairs={{0,4},{4,0},{8,12},{12,8},{16,20},{20,16},{24,28},{28,24},{1,5},{5... | collective-permute-start | bytes 2064392 | tf_op jit(solution)/shard_map/ppermute | solution.py:355
  62.5 8.7 %collective-permute-start = (bf16[2,16,768]{2,1,0:T(8,128)(2,1)S(1)}, bf16[2,16,768]{2,1,0:T(8,128)(2,1)S(1)}, u32[]{:S(2)}, u32[]{:S(2)}) collective-permute-start(bf16[2,16,768]{2,1,0:T(8,128)(2,1)S(1)} %slice.99), channel_id=1, source_target_pairs={{0,1},{1,2},{2,3},{3,4},{4,5},{5,6},{6,7},{7,8},{8,9},{9,10},{10,1... | collective-permute-start | bytes 147464 | tf_op jit(solution)/shard_map/ppermute | solution.py:560
  71.3 1.1 copy-start.13
  112.2 7.1 %copy-start.27 = (f32[24]{0:T(128)S(1)}, f32[24]{0:T(128)}, u32[]{:S(2)}) copy-start(f32[24]{0:T(128)} %param.19) | copy-start | bytes 292
  112.2 7.8 %copy-start.22 = (f32[1536]{0:T(1024)S(1)}, f32[1536]{0:T(1024)}, u32[]{:S(2)}) copy-start(f32[1536]{0:T(1024)} %param.20) | copy-start | bytes 18436
  112.2 8.4 %copy-start.7 = (f32[2,256,128]{2,1,0:T(8,128)S(1)}, f32[2,256,128]{2,1,0:T(8,128)}, u32[]{:S(2)}) copy-start(f32[2,256,128]{2,1,0:T(8,128)} %get-tuple-element.42.step) | copy-start | bytes 786436
  114.8 24.0 %all-to-all-start.1 = ((bf16[32,8,1536]{2,1,0:T(8,128)(2,1)}), bf16[32,8,1536]{2,1,0:T(8,128)(2,1)S(1)}, u32[]{:S(2)}, u32[]{:S(2)}) async-start(bf16[32,8,1536]{2,1,0:T(8,128)(2,1)} %state_scan.2), calls=%async_computation.1 | async-start | bytes 1572864 | tf_op jit(solution)/shard_map/all_to_all | solution.py:498
  121.5 5.4 %copy-start.11 = (bf16[2,256,768]{2,1,0:T(8,128)(2,1)S(1)}, bf16[2,256,768]{2,1,0:T(8,128)(2,1)}, u32[]{:S(2)}) copy-start(bf16[2,256,768]{2,1,0:T(8,128)(2,1)} %get-tuple-element.44) | copy-start | bytes 2359300
  126.9 4.9 %copy-start.10 = (bf16[2,256,768]{2,1,0:T(8,128)(2,1)S(1)}, bf16[2,256,768]{2,1,0:T(8,128)(2,1)}, u32[]{:S(2)}) copy-start(bf16[2,256,768]{2,1,0:T(8,128)(2,1)} %param.12) | copy-start | bytes 2359300
  126.9 4.8 %copy-start.28 = (bf16[768,3072]{1,0:T(8,128)(2,1)S(1)}, bf16[768,3072]{1,0:T(8,128)(2,1)}, u32[]{:S(2)}) copy-start(bf16[768,3072]{1,0:T(8,128)(2,1)} %all-gather.2.cloned.1.call-done) | copy-start | bytes 14155780
  155.0 25.3 %all-to-all-start.2 = ((bf16[32,8,1664]{2,1,0:T(8,128)(2,1)}), bf16[32,8,1664]{2,1,0:T(8,128)(2,1)S(1)}, u32[]{:S(2)}, u32[]{:S(2)}) async-start(bf16[32,8,1664]{2,1,0:T(8,128)(2,1)} %bitcast.12), calls=%async_computation.2 | async-start | bytes 1703936 | tf_op jit(solution)/shard_map/all_to_all | solution.py:472
  159.4 121.1 %reduce-scatter.3.cloned.1.call-start = ((), (), s32[]{:S(2)}) async-start(), calls=%async_computation.7 | async-start | bytes 5308416 | tf_op jit(solution)/shard_map/reduce_scatter | solution.py:514
  159.4 3.0 copy-start.8
  165.2 23.3 %copy-start = (bf16[2,256,768]{2,1,0:T(8,128)(2,1)S(1)}, bf16[2,256,768]{2,1,0:T(8,128)(2,1)}, u32[]{:S(2)}) copy-start(bf16[2,256,768]{2,1,0:T(8,128)(2,1)} %hid.1) | copy-start | bytes 2359300
  180.3 0.9 copy-start.2
  183.8 24.0 %all-to-all-start.3 = ((bf16[32,8,1536]{2,1,0:T(8,128)(2,1)}), bf16[32,8,1536]{2,1,0:T(8,128)(2,1)S(1)}, u32[]{:S(2)}, u32[]{:S(2)}) async-start(bf16[32,8,1536]{2,1,0:T(8,128)(2,1)} %state_scan.3), calls=%async_computation.3 | async-start | bytes 1572864 | tf_op jit(solution)/shard_map/all_to_all | solution.py:498
  188.2 115.3 %reduce-scatter.5.cloned.1.call-start = ((), (), s32[]{:S(2)}) async-start(), calls=%async_computation.8 | async-start | bytes 737280 | tf_op jit(solution)/shard_map/reduce_scatter | solution.py:515
  188.8 9.6 %copy-start.18 = (f32[2,8,1536]{2,1,0:T(8,128)S(1)}, f32[2,8,1536]{2,1,0:T(8,128)}, u32[]{:S(2)}) copy-start(f32[2,8,1536]{2,1,0:T(8,128)} %get-tuple-element.61) | copy-start | bytes 294916
  207.8 0.9 copy-start.3
  208.7 17.4 %copy-start.5 = (bf16[768,1920]{1,0:T(8,128)(2,1)S(1)}, bf16[768,1920]{1,0:T(8,128)(2,1)}, u32[]{:S(2)}) copy-start(bf16[768,1920]{1,0:T(8,128)(2,1)} %get-tuple-element.57) | copy-start | bytes 8847364
  226.1 8.2 %copy-start.9 = (bf16[2,256,1920]{2,1,0:T(8,128)(2,1)S(1)}, bf16[2,256,1920]{2,1,0:T(8,128)(2,1)}, u32[]{:S(2)}) copy-start(bf16[2,256,1920]{2,1,0:T(8,128)(2,1)} %get-tuple-element.56) | copy-start | bytes 5898244
  228.6 12.7 %collective-permute-start.13 = (f32[2,8,768]{2,1,0:T(8,128)}, f32[2,8,768]{2,1,0:T(8,128)}, u32[]{:S(2)}, u32[]{:S(2)}) collective-permute-start(f32[2,8,768]{2,1,0:T(8,128)} %fusion.1), channel_id=1, source_target_pairs={{1,0},{2,1},{3,2},{4,3},{5,4},{6,5},{7,6},{8,7},{9,8},{10,9},{11,1... | collective-permute-start | bytes 147464 | tf_op jit(solution)/shard_map/ppermute | solution.py:699
  234.3 3.8 %copy-start.29 = (bf16[2,256,1536]{2,1,0:T(8,128)(2,1)S(1)}, bf16[2,256,1536]{2,1,0:T(8,128)(2,1)}, u32[]{:S(2)}) copy-start(bf16[2,256,1536]{2,1,0:T(8,128)(2,1)} %get-tuple-element.46) | copy-start | bytes 4718596
  238.0 3.2 %copy-start.17 = (f32[8,1792]{1,0:T(8,128)S(1)}, f32[8,1792]{1,0:T(8,128)}, u32[]{:S(2)}) copy-start(f32[8,1792]{1,0:T(8,128)} %reduce_sum.66) | copy-start | bytes 172036
  238.1 3.2 %slice-start = ((f32[8,1792]{1,0:T(8,128)}), f32[4,1792]{1,0:T(4,128)S(1)}, s32[]{:S(2)}) async-start(f32[8,1792]{1,0:T(8,128)} %reduce_sum.66), calls=%async_computation.9 | async-start | bytes 57344 | tf_op jit(solution)/shard_map/slice | solution.py:719
  241.3 1.4 copy-start.24
  241.3 1.4 copy-start.25
  241.3 1.4 copy-start.26
  242.8 4.9 %collective-permute-start.14 = (f32[12288]{0:T(1024)S(1)}, f32[12288]{0:T(1024)S(1)}, u32[]{:S(2)}, u32[]{:S(2)}) collective-permute-start(f32[12288]{0:T(1024)S(1)} %pad.28), channel_id=1, source_target_pairs={{0,4},{4,0},{8,12},{12,8},{16,20},{20,16},{24,28},{28,24},{1,5},{5... | collective-permute-start | bytes 147464 | tf_op jit(solution)/shard_map/ppermute | solution.py:355
  247.7 8.4 %collective-permute-start.15 = (f32[12288]{0:T(1024)S(1)}, f32[12288]{0:T(1024)S(1)}, u32[]{:S(2)}, u32[]{:S(2)}) collective-permute-start(f32[12288]{0:T(1024)S(1)} %pad_add_fusion.1), channel_id=1, source_target_pairs={{0,8},{4,12},{8,0},{12,4},{16,24},{20,28},{24,16},{28,20},{1,9},{5... | collective-permute-start | bytes 147464 | tf_op jit(solution)/shard_map/ppermute | solution.py:355
  255.4 10.5 %collective-permute-start.19 = (bf16[384,896]{1,0:T(8,128)(2,1)}, bf16[384,896]{1,0:T(8,128)(2,1)}, u32[]{:S(2)}, u32[]{:S(2)}) collective-permute-start(bf16[384,896]{1,0:T(8,128)(2,1)} %get-tuple-element.64), channel_id=1, source_target_pairs={{0,4},{4,0},{8,12},{12,8},{16,20},{20,16},{24,28},{28,24},{1,5},{5... | collective-permute-start | bytes 2064392 | tf_op jit(solution)/shard_map/ppermute | solution.py:355
  255.7 12.6 %collective-permute-start.22 = (bf16[384,1024]{1,0:T(8,128)(2,1)}, bf16[384,1024]{1,0:T(8,128)(2,1)S(1)}, u32[]{:S(2)}, u32[]{:S(2)}) collective-permute-start(bf16[384,1024]{1,0:T(8,128)(2,1)} %get-tuple-element.66), channel_id=1, source_target_pairs={{0,4},{4,0},{8,12},{12,8},{16,20},{20,16},{24,28},{28,24},{1,5},{5... | collective-permute-start | bytes 2359304 | tf_op jit(solution)/shard_map/ppermute | solution.py:355
  256.0 9.9 %copy-start.14 = (bf16[384,896]{1,0:T(8,128)(2,1)S(1)}, bf16[384,896]{1,0:T(8,128)(2,1)}, u32[]{:S(2)}) copy-start(bf16[384,896]{1,0:T(8,128)(2,1)} %get-tuple-element.63) | copy-start | bytes 2064388
  256.0 5.1 %collective-permute-start.16 = (f32[12288]{0:T(1024)S(1)}, f32[12288]{0:T(1024)S(1)}, u32[]{:S(2)}, u32[]{:S(2)}) collective-permute-start(f32[12288]{0:T(1024)S(1)} %add.114), channel_id=1, source_target_pairs={{0,16},{4,20},{8,24},{12,28},{16,0},{20,4},{24,8},{28,12},{1,17},{... | collective-permute-start | bytes 147464 | tf_op jit(solution)/shard_map/ppermute | solution.py:355
  261.1 7.1 %copy-start.12 = (bf16[384,1024]{1,0:T(8,128)(2,1)S(1)}, bf16[384,1024]{1,0:T(8,128)(2,1)}, u32[]{:S(2)}) copy-start(bf16[384,1024]{1,0:T(8,128)(2,1)} %get-tuple-element.65) | copy-start | bytes 2359300
  261.2 4.2 %collective-permute-start.17 = (f32[12288]{0:T(1024)S(1)}, f32[12288]{0:T(1024)S(1)}, u32[]{:S(2)}, u32[]{:S(2)}) collective-permute-start(f32[12288]{0:T(1024)S(1)} %add.115), channel_id=1, source_target_pairs={{0,1},{1,0},{2,3},{3,2},{4,5},{5,4},{6,7},{7,6},{8,9},{9,8},{10,11... | collective-permute-start | bytes 147464 | tf_op jit(solution)/shard_map/ppermute | solution.py:355
  265.3 7.6 %collective-permute-start.18 = (f32[12288]{0:T(1024)S(1)}, f32[12288]{0:T(1024)S(1)}, u32[]{:S(2)}, u32[]{:S(2)}) collective-permute-start(f32[12288]{0:T(1024)S(1)} %add.116), channel_id=1, source_target_pairs={{0,2},{1,3},{2,0},{3,1},{4,6},{5,7},{6,4},{7,5},{8,10},{9,11},{10,... | collective-permute-start | bytes 147464 | tf_op jit(solution)/shard_map/ppermute | solution.py:355
  267.3 8.4 %collective-permute-start.20 = (bf16[192,896]{1,0:T(8,128)(2,1)S(1)}, bf16[192,896]{1,0:T(8,128)(2,1)S(1)}, u32[]{:S(2)}, u32[]{:S(2)}) collective-permute-start(bf16[192,896]{1,0:T(8,128)(2,1)S(1)} %slice.143), channel_id=1, source_target_pairs={{0,16},{4,20},{8,24},{12,28},{16,0},{20,4},{24,8},{28,12},{1,17},{... | collective-permute-start | bytes 1032200 | tf_op jit(solution)/shard_map/ppermute | solution.py:355
  268.6 11.4 %collective-permute-start.23 = (bf16[192,1024]{1,0:T(8,128)(2,1)S(1)}, bf16[192,1024]{1,0:T(8,128)(2,1)S(1)}, u32[]{:S(2)}, u32[]{:S(2)}) collective-permute-start(bf16[192,1024]{1,0:T(8,128)(2,1)S(1)} %slice.147), channel_id=1, source_target_pairs={{0,8},{4,12},{8,0},{12,4},{16,24},{20,28},{24,16},{28,20},{1,9},{5... | collective-permute-start | bytes 1179656 | tf_op jit(solution)/shard_map/ppermute | solution.py:355
  275.8 6.0 %collective-permute-start.21 = (bf16[96,896]{1,0:T(8,128)(2,1)S(1)}, bf16[96,896]{1,0:T(8,128)(2,1)S(1)}, u32[]{:S(2)}, u32[]{:S(2)}) collective-permute-start(bf16[96,896]{1,0:T(8,128)(2,1)S(1)} %slice.145), channel_id=1, source_target_pairs={{0,8},{4,12},{8,0},{12,4},{16,24},{20,28},{24,16},{28,20},{1,9},{5... | collective-permute-start | bytes 516104 | tf_op jit(solution)/shard_map/ppermute | solution.py:355
  280.1 5.7 %collective-permute-start.24 = (bf16[96,1024]{1,0:T(8,128)(2,1)S(1)}, bf16[96,1024]{1,0:T(8,128)(2,1)S(1)}, u32[]{:S(2)}, u32[]{:S(2)}) collective-permute-start(bf16[96,1024]{1,0:T(8,128)(2,1)S(1)} %slice.149), channel_id=1, source_target_pairs={{0,16},{4,20},{8,24},{12,28},{16,0},{20,4},{24,8},{28,12},{1,17},{... | collective-permute-start | bytes 589832 | tf_op jit(solution)/shard_map/ppermute | solution.py:355
  285.9 8.7 %collective-permute-start.25 = (bf16[24,1920]{1,0:T(8,128)(2,1)S(1)}, bf16[24,1920]{1,0:T(8,128)(2,1)S(1)}, u32[]{:S(2)}, u32[]{:S(2)}) collective-permute-start(bf16[24,1920]{1,0:T(8,128)(2,1)S(1)} %get-tuple-element.71), channel_id=1, source_target_pairs={{0,1},{1,2},{2,3},{3,0},{4,5},{5,6},{6,7},{7,4},{8,9},{9,10},{10,1... | collective-permute-start | bytes 276488 | tf_op jit(solution)/shard_map/ppermute | solution.py:431
  286.9 11.3 %collective-permute-start.26 = (bf16[24,1920]{1,0:T(8,128)(2,1)S(1)}, bf16[24,1920]{1,0:T(8,128)(2,1)S(1)}, u32[]{:S(2)}, u32[]{:S(2)}) collective-permute-start(bf16[24,1920]{1,0:T(8,128)(2,1)S(1)} %get-tuple-element.72), channel_id=1, source_target_pairs={{0,2},{1,3},{2,0},{3,1},{4,6},{5,7},{6,4},{7,5},{8,10},{9,11},{10,... | collective-permute-start | bytes 276488 | tf_op jit(solution)/shard_map/ppermute | solution.py:431
  288.9 9.9 %collective-permute-start.27 = (bf16[24,1920]{1,0:T(8,128)(2,1)S(1)}, bf16[24,1920]{1,0:T(8,128)(2,1)S(1)}, u32[]{:S(2)}, u32[]{:S(2)}) collective-permute-start(bf16[24,1920]{1,0:T(8,128)(2,1)S(1)} %get-tuple-element.73), channel_id=1, source_target_pairs={{0,3},{1,0},{2,1},{3,2},{4,7},{5,4},{6,5},{7,6},{8,11},{9,8},{10,9... | collective-permute-start | bytes 276488 | tf_op jit(solution)/shard_map/ppermute | solution.py:431
  (3 other events, 2.3 us)
Sparse Core Ops, SparseCore 0:
  28.7 44.7 all-gather.1
  165.3 63.4 reduce-scatter.2
  280.6 22.8 reduce-scatter.4
